TPU v7x, 128 devices: a whole 4x4x4 slice. The times are simulated.
128 devices in a mesh: wide: 32 (over y, z, core), narrow: 4 (over x).
Axes of the slice: x: 4, y: 4, z: 4, core: 2. Of those that a mesh axis runs over, the one named last changes fastest.
Arguments:
- frames_lr: float32 [4, 256, 128, 128], P('narrow', 'wide'), may hold values from -24 to 24
- anchor_col: int32 [4, 256], P('narrow'), may hold values from 0 to 31, as said below
- shift_index: int32 [4, 256, 2], P('narrow'), may hold values from 0 to 15
- initial_guess: float32 [2048, 16384], P('narrow', 'wide'), may hold values from -6 to 6
Outputs:
- solution: float32 [2048, 16384], P('narrow', 'wide')
- residual: float32 [2048, 16384], P('narrow', 'wide')
Inputs may be any that keep to these rules, and one draw needn't show every extreme that they name: `anchor_col`: frame f's anchor column differs from its owner column f // 8 by at most one.
All inputs are finite; a program needn't handle non-finite values.
Results may differ from a plain program's by a relative error of at most 0.0003.
Values sent between devices are 32-bit elements; how exact they have to be, the bound alone decides.
A program may use at most 64 MiB of HBM per device.

v0:
```python
import jax
import jax.numpy as jnp
from jax import lax
from jax.sharding import PartitionSpec as P

NSHIFT = 16
ITERS = 2


highest = lax.Precision.HIGHEST
damping = 0.05


def with_halo(shard, sides, width):
    for axis, dim in sides:
        count, length = (lax.axis_size(axis), shard.shape[dim])
        up = [(i, (i + 1) % count) for i in range(count - 1)]
        down = [(j, i) for i, j in up]
        last = lax.slice_in_dim(shard, length - width, length, axis=dim)
        leading = lax.slice_in_dim(shard, 0, width, axis=dim)
        before = lax.ppermute(last, axis, up)
        after = lax.ppermute(leading, axis, down)
        shard = jnp.concatenate([before, shard, after], axis=dim)
    return shard


def tap_table():
    fraction = jnp.arange(NSHIFT, dtype=jnp.float32) / NSHIFT
    offsets = jnp.arange(8, dtype=jnp.float32)[None, :] - 3.0 - fraction[:, None]
    lanczos = jnp.sinc(offsets) * jnp.sinc(offsets / 4.0)
    lanczos = lanczos / jnp.sum(lanczos, axis=1, keepdims=True)
    spread = jnp.arange(11)[None, :] - jnp.arange(8)[:, None]
    blur = jnp.where((spread >= 0) & (spread < 4), 0.25, 0.0).astype(jnp.float32)
    return jnp.dot(lanczos, blur, precision=highest, preferred_element_type=jnp.float32)


def operator_matrix(tap_rows, index, low_size, high_size):
    weights = tap_rows[index]
    offsets = jnp.arange(high_size)[None, :] - 4 * jnp.arange(low_size)[:, None]
    matrix = jnp.zeros((low_size, high_size), jnp.float32)
    for place in range(11):
        matrix = matrix + jnp.where(offsets == place, weights[place], 0.0)
    return matrix


def frame_pass(window, observed, tap_rows, kernels):
    low_size = observed.shape[0]
    high_size = window.shape[0]
    row_map = operator_matrix(tap_rows, kernels[0], low_size, high_size)
    col_map = operator_matrix(tap_rows, kernels[1], low_size, high_size)
    model = jnp.dot(
        jnp.dot(row_map, window, precision=highest, preferred_element_type=jnp.float32),
        col_map.T,
        precision=highest,
        preferred_element_type=jnp.float32,
    )
    mismatch = model - observed
    right = jnp.dot(mismatch, col_map, precision=highest, preferred_element_type=jnp.float32)
    return jnp.dot(row_map.T, right, precision=highest, preferred_element_type=jnp.float32)


def fold_rows(extended):
    size = extended.shape[0] - 16
    core = extended[8 : size + 8]
    upper = jnp.pad(extended[0:4], ((0, size - 4), (0, 0)))
    lower = jnp.pad(extended[size + 12 :], ((size - 4, 0), (0, 0)))
    return core + upper + lower


def fold_cols(extended):
    size = extended.shape[1] - 16
    core = extended[:, 8 : size + 8]
    left_part = jnp.pad(extended[:, 0:4], ((0, 0), (0, size - 4)))
    right_part = jnp.pad(extended[:, size + 12 :], ((0, 0), (size - 4, 0)))
    return core + left_part + right_part


def extend(vector):
    return with_halo(vector, (("wide", 1), ("narrow", 0)), 4)


def settle(gathered):
    extended = with_halo(gathered, (("wide", 1), ("narrow", 0)), 4)
    return fold_cols(fold_rows(extended))


def squares(vector):
    return lax.psum(jnp.sum(vector * vector), ("wide", "narrow"))


def on_device(frames_lr, anchor_col, shift_index, initial_guess):
    tap_rows = tap_table()
    column = lax.axis_index("wide")
    observed_all = frames_lr[0]
    per_owner = observed_all.shape[0]
    extent = initial_guess.shape[0] + 8
    own_codes = lax.dynamic_slice_in_dim(anchor_col[0], column * per_owner, per_owner)
    own_kernels = lax.dynamic_slice_in_dim(shift_index[0], column * per_owner, per_owner, 0)

    def normal_pass(vector, scale_data):
        edges = extend(vector)
        strip = with_halo(edges, (("wide", 1),), extent)

        def accumulate(total, record):
            observed, anchor, kernels = record
            start = (anchor - column + 1) * extent
            window = lax.dynamic_slice_in_dim(strip, start, extent, 1)
            current = lax.dynamic_slice_in_dim(total, start, extent, 1)
            contrib = frame_pass(window, scale_data * observed, tap_rows, kernels)
            return (lax.dynamic_update_slice_in_dim(total, current + contrib, start, 1), None)

        total, _ = lax.scan(
            accumulate,
            jnp.zeros((extent, 3 * extent), jnp.float32),
            (observed_all, own_codes, own_kernels),
        )
        outer = jnp.concatenate([total[:, :extent], total[:, 2 * extent :]], axis=1)
        returned = with_halo(outer, (("wide", 1),), extent)
        gathered = total[:, extent : 2 * extent] + returned[:, :extent] + returned[:, 3 * extent :]
        return settle(gathered)

    solution = initial_guess
    residual = -(normal_pass(initial_guess, 1.0) + damping * initial_guess)
    direction = residual
    norm_now = squares(residual)
    for step in range(ITERS):
        image = normal_pass(direction, 0.0) + damping * direction
        alpha = norm_now / lax.psum(jnp.sum(direction * image), ("wide", "narrow"))
        solution = solution + alpha * direction
        residual = residual - alpha * image
        norm_next = squares(residual)
        direction = residual + norm_next / norm_now * direction
        norm_now = norm_next
    return (solution, residual)


def solution(mesh):
    placed = (
        P("narrow", "wide", None, None),
        P("narrow", None),
        P("narrow", None, None),
        P("narrow", "wide"),
    )
    return jax.shard_map(
        on_device,
        mesh=mesh,
        in_specs=placed,
        out_specs=(P("narrow", "wide"), P("narrow", "wide")),
        check_vma=False,
    )
```

profile of v0, /device:TPU:1, one launch (start us, length us, event | category | flops | bytes accessed | tf_op | source)
XLA Modules:
  0.0 1746.9 jit_solution(9258231831784794111)
XLA Ops:
  28.9 13.1 collective-permute-done.5
  49.5 404.0 %while.30 = (s32[]{:T(128)}, f32[520,1560]{1,0:T(8,128)}, s32[8]{0:T(128)S(1)}, s32[]{:T(128)}, s32[8,2]{0,1:T(2,128)S(1)}, /*index=5*/f32[16,11]{1,0:T(8,128)S(...) while((s32[]{:T(128)}, f32[520,1560]{1,0:T(8,128)}, ...), condition=%wide.region_2.4_spmd, body=%wide.region_1.3_spmd.sunk | while | flops 1044213952 | bytes 6928187 | solution.py:112
  56.6 10.1 fusion.332
  83.0 10.2 convolution_add_fusion.6
  107.4 10.0 fusion.332
  133.6 10.1 convolution_add_fusion.6
  157.8 10.0 fusion.332
  184.1 10.1 convolution_add_fusion.6
  208.3 10.0 fusion.332
  234.5 10.1 convolution_add_fusion.6
  258.8 10.0 fusion.332
  285.0 10.1 convolution_add_fusion.6
  309.2 10.0 fusion.332
  335.5 10.1 convolution_add_fusion.6
  359.7 10.0 fusion.332
  385.9 10.1 convolution_add_fusion.6
  410.2 10.0 fusion.332
  436.4 10.1 convolution_add_fusion.6
  464.4 12.8 collective-permute-done.6
  529.8 13.4 collective-permute-done.17
  550.7 404.2 %while.31 = (s32[]{:T(128)}, f32[520,1560]{1,0:T(8,128)}, s32[8]{0:T(128)S(1)}, s32[]{:T(128)}, s32[8,2]{0,1:T(2,128)S(1)}, /*index=5*/f32[16,11]{1,0:T(8,128)S(...) while((s32[]{:T(128)}, f32[520,1560]{1,0:T(8,128)}, ...), condition=%wide.region_6.8_spmd, body=%wide.region_5.7_spmd.sunk | while | flops 1044230336 | bytes 6928187 | solution.py:112
  557.8 10.1 fusion.341
  584.2 10.2 convolution_add_fusion.7
  608.5 10.0 fusion.341
  634.8 10.1 convolution_add_fusion.7
  659.0 10.0 fusion.341
  669.1 8.6 convolution_subtract_fusion.7
  685.3 10.1 convolution_add_fusion.7
  709.5 10.0 fusion.341
  735.8 10.2 convolution_add_fusion.7
  760.0 10.0 fusion.341
  770.0 8.6 convolution_subtract_fusion.7
  786.3 10.1 convolution_add_fusion.7
  810.5 10.0 fusion.341
  836.8 10.1 convolution_add_fusion.7
  861.0 10.0 fusion.341
  871.0 8.6 convolution_subtract_fusion.7
  887.3 10.1 convolution_add_fusion.7
  911.5 10.0 fusion.341
  937.7 10.2 convolution_add_fusion.7
  965.7 12.8 collective-permute-done.18
  990.2 10.4 collective-permute-done.21
  1007.9 83.4 %all-reduce.9 = (f32[]{:T(128)}, f32[]{:T(128)}) all-reduce(f32[]{:T(128)} %get-tuple-element.133, f32[]{:T(128)} %get-tuple-element.132), channel_id=1, replica_groups=mesh['wide'=32,'narrow'=4] {'wide','narrow'}, use_global_device_ids=true, to_apply=%region_4.6 | all-reduce | flops 2 | bytes 16 | tf_op jit(solution)/shard_map/psum | solution.py:88
  1094.8 72.0 %psum.30 = f32[]{:T(128)} all-reduce(f32[]{:T(128)} %get-tuple-element.184), channel_id=1, replica_groups=mesh['wide'=32,'narrow'=4] {'wide','narrow'}, use_global_device_ids=true, to_apply=%region_10.12 | all-reduce | flops 1 | bytes 8 | tf_op jit(solution)/shard_map/psum | solution.py:88
  1191.7 13.7 collective-permute-done.29
  1212.9 401.1 %while.32 = (s32[]{:T(128)}, f32[520,1560]{1,0:T(8,128)}, s32[8]{0:T(128)S(1)}, s32[]{:T(128)}, s32[8,2]{0,1:T(2,128)S(1)}, /*index=5*/f32[16,11]{1,0:T(8,128)S(...) while((s32[]{:T(128)}, f32[520,1560]{1,0:T(8,128)}, ...), condition=%wide.region_12.14_spmd, body=%wide.region_11.13_spmd.sunk | while | flops 1044230336 | bytes 6928187 | solution.py:112
  1219.8 10.1 fusion.350
  1246.0 10.2 convolution_add_fusion.8
  1270.1 10.0 fusion.350
  1296.3 10.1 convolution_add_fusion.8
  1320.2 10.0 fusion.350
  1346.4 10.1 convolution_add_fusion.8
  1370.3 10.0 fusion.350
  1396.5 10.1 convolution_add_fusion.8
  1420.4 10.0 fusion.350
  1446.6 10.1 convolution_add_fusion.8
  1470.5 10.0 fusion.350
  1496.7 10.1 convolution_add_fusion.8
  1520.6 10.0 fusion.350
  1546.8 10.1 convolution_add_fusion.8
  1570.7 10.0 fusion.350
  1596.9 10.1 convolution_add_fusion.8
  1624.8 12.8 collective-permute-done.30
  1665.7 76.2 %psum.31 = f32[]{:T(128)} all-reduce(f32[]{:T(128)} %multiply_reduce_fusion), channel_id=1, replica_groups=mesh['wide'=32,'narrow'=4] {'wide','narrow'}, use_global_device_ids=true, to_apply=%region_14.16 | all-reduce | flops 1 | bytes 8 | tf_op jit(solution)/shard_map/psum | solution.py:128
  (366 shorter events, 806.2 us)
Async XLA Ops:
  0.6 27.8 %copy-start = (s32[1,256,2]{1,2,0:T(2,128)S(1)}, s32[1,256,2]{1,2,0:T(2,128)}, u32[]{:S(2)}) copy-start(s32[1,256,2]{1,2,0:T(2,128)} %param.13) | copy-start | bytes 6148
  0.6 13.9 copy-start.2
  1.9 8.2 collective-permute-start
  6.9 7.7 collective-permute-start.1
  14.6 4.4 collective-permute-start.2
  17.7 10.6 copy-start.7
  17.8 4.4 collective-permute-start.3
  22.7 19.3 %collective-permute-start.5 = (f32[520,520]{1,0:T(8,128)S(1)}, f32[520,520]{1,0:T(8,128)}, u32[]{:S(2)}, u32[]{:S(2)}) collective-permute-start(f32[520,520]{1,0:T(8,128)S(1)} %pad_maximum_fusion), channel_id=1, source_target_pairs={{4,0},{8,4},{12,8},{16,12},{20,16},{24,20},{28,24},{32,28},{36,32}... | collective-permute-start | bytes 3244808 | tf_op jit(solution)/shard_map/ppermute | solution.py:22
  24.6 18.4 %collective-permute-start.4 = (f32[520,520]{1,0:T(8,128)S(1)}, f32[520,520]{1,0:T(8,128)}, u32[]{:S(2)}, u32[]{:S(2)}) collective-permute-start(f32[520,520]{1,0:T(8,128)S(1)} %pad_maximum_fusion), channel_id=1, source_target_pairs={{0,4},{4,8},{8,12},{12,16},{16,20},{20,24},{24,28},{28,32},{32,36}... | collective-permute-start | bytes 3244808 | tf_op jit(solution)/shard_map/ppermute | solution.py:21
  455.7 21.5 %collective-permute-start.6 = (f32[520,520]{1,0:T(8,128)S(1)}, f32[520,520]{1,0:T(8,128)S(1)}, u32[]{:S(2)}, u32[]{:S(2)}) collective-permute-start(f32[520,520]{1,0:T(8,128)S(1)} %get-tuple-element.270), channel_id=1, source_target_pairs={{0,4},{4,8},{8,12},{12,16},{16,20},{20,24},{24,28},{28,32},{32,36}... | collective-permute-start | bytes 3244808 | tf_op jit(solution)/shard_map/ppermute | solution.py:21
  462.4 19.1 %collective-permute-start.7 = (f32[520,520]{1,0:T(8,128)S(1)}, f32[520,520]{1,0:T(8,128)S(1)}, u32[]{:S(2)}, u32[]{:S(2)}) collective-permute-start(f32[520,520]{1,0:T(8,128)S(1)} %get-tuple-element.271), channel_id=1, source_target_pairs={{4,0},{8,4},{12,8},{16,12},{20,16},{24,20},{28,24},{32,28},{36,32}... | collective-permute-start | bytes 3244808 | tf_op jit(solution)/shard_map/ppermute | solution.py:22
  483.6 5.3 collective-permute-start.8
  485.5 10.6 collective-permute-start.9
  496.2 3.1 collective-permute-start.10
  497.5 6.3 collective-permute-start.11
  499.3 4.7 copy-start.6
  504.6 6.2 collective-permute-start.12
  507.5 7.7 collective-permute-start.13
  515.3 4.9 collective-permute-start.14
  518.9 4.4 collective-permute-start.15
  523.9 19.3 %collective-permute-start.17 = (f32[520,520]{1,0:T(8,128)S(1)}, f32[520,520]{1,0:T(8,128)}, u32[]{:S(2)}, u32[]{:S(2)}) collective-permute-start(f32[520,520]{1,0:T(8,128)S(1)} %pad_maximum_fusion.2), channel_id=1, source_target_pairs={{4,0},{8,4},{12,8},{16,12},{20,16},{24,20},{28,24},{32,28},{36,32}... | collective-permute-start | bytes 3244808 | tf_op jit(solution)/shard_map/ppermute | solution.py:22
  525.8 18.4 %collective-permute-start.16 = (f32[520,520]{1,0:T(8,128)S(1)}, f32[520,520]{1,0:T(8,128)}, u32[]{:S(2)}, u32[]{:S(2)}) collective-permute-start(f32[520,520]{1,0:T(8,128)S(1)} %pad_maximum_fusion.2), channel_id=1, source_target_pairs={{0,4},{4,8},{8,12},{12,16},{16,20},{20,24},{24,28},{28,32},{32,36}... | collective-permute-start | bytes 3244808 | tf_op jit(solution)/shard_map/ppermute | solution.py:21
  957.0 21.5 %collective-permute-start.18 = (f32[520,520]{1,0:T(8,128)S(1)}, f32[520,520]{1,0:T(8,128)S(1)}, u32[]{:S(2)}, u32[]{:S(2)}) collective-permute-start(f32[520,520]{1,0:T(8,128)S(1)} %get-tuple-element.268), channel_id=1, source_target_pairs={{0,4},{4,8},{8,12},{12,16},{16,20},{20,24},{24,28},{28,32},{32,36}... | collective-permute-start | bytes 3244808 | tf_op jit(solution)/shard_map/ppermute | solution.py:21
  963.8 19.1 %collective-permute-start.19 = (f32[520,520]{1,0:T(8,128)S(1)}, f32[520,520]{1,0:T(8,128)S(1)}, u32[]{:S(2)}, u32[]{:S(2)}) collective-permute-start(f32[520,520]{1,0:T(8,128)S(1)} %get-tuple-element.269), channel_id=1, source_target_pairs={{4,0},{8,4},{12,8},{16,12},{20,16},{24,20},{28,24},{32,28},{36,32}... | collective-permute-start | bytes 3244808 | tf_op jit(solution)/shard_map/ppermute | solution.py:22
  984.9 5.3 collective-permute-start.20
  986.8 13.7 collective-permute-start.21
  1000.7 3.1 collective-permute-start.22
  1002.0 4.4 collective-permute-start.23
  1006.6 1.3 copy-start.5
  1094.8 73.5 %copy-start.3 = (f32[512,512]{1,0:T(8,128)}, f32[512,512]{1,0:T(8,128)S(1)}, u32[]{:S(2)}) copy-start(f32[512,512]{1,0:T(8,128)S(1)} %get-tuple-element.185) | copy-start | bytes 3145732
  1168.5 6.8 collective-permute-start.24
  1172.0 7.7 collective-permute-start.25
  1179.7 2.6 collective-permute-start.26
  1181.0 4.6 collective-permute-start.27
  1186.1 19.3 %collective-permute-start.29 = (f32[520,520]{1,0:T(8,128)S(1)}, f32[520,520]{1,0:T(8,128)}, u32[]{:S(2)}, u32[]{:S(2)}) collective-permute-start(f32[520,520]{1,0:T(8,128)S(1)} %pad_maximum_fusion.4), channel_id=1, source_target_pairs={{4,0},{8,4},{12,8},{16,12},{20,16},{24,20},{28,24},{32,28},{36,32}... | collective-permute-start | bytes 3244808 | tf_op jit(solution)/shard_map/ppermute | solution.py:22
  1188.0 18.4 %collective-permute-start.28 = (f32[520,520]{1,0:T(8,128)S(1)}, f32[520,520]{1,0:T(8,128)}, u32[]{:S(2)}, u32[]{:S(2)}) collective-permute-start(f32[520,520]{1,0:T(8,128)S(1)} %pad_maximum_fusion.4), channel_id=1, source_target_pairs={{0,4},{4,8},{8,12},{12,16},{16,20},{20,24},{24,28},{28,32},{32,36}... | collective-permute-start | bytes 3244808 | tf_op jit(solution)/shard_map/ppermute | solution.py:21
  1616.1 21.5 %collective-permute-start.30 = (f32[520,520]{1,0:T(8,128)S(1)}, f32[520,520]{1,0:T(8,128)S(1)}, u32[]{:S(2)}, u32[]{:S(2)}) collective-permute-start(f32[520,520]{1,0:T(8,128)S(1)} %get-tuple-element.266), channel_id=1, source_target_pairs={{0,4},{4,8},{8,12},{12,16},{16,20},{20,24},{24,28},{28,32},{32,36}... | collective-permute-start | bytes 3244808 | tf_op jit(solution)/shard_map/ppermute | solution.py:21
  1622.9 19.1 %collective-permute-start.31 = (f32[520,520]{1,0:T(8,128)S(1)}, f32[520,520]{1,0:T(8,128)S(1)}, u32[]{:S(2)}, u32[]{:S(2)}) collective-permute-start(f32[520,520]{1,0:T(8,128)S(1)} %get-tuple-element.267), channel_id=1, source_target_pairs={{4,0},{8,4},{12,8},{16,12},{20,16},{24,20},{28,24},{32,28},{36,32}... | collective-permute-start | bytes 3244808 | tf_op jit(solution)/shard_map/ppermute | solution.py:22
  1644.1 5.3 collective-permute-start.32
  1646.0 10.5 collective-permute-start.33
  1656.5 3.1 collective-permute-start.34
  1657.8 5.9 collective-permute-start.35
  1664.0 0.7 copy-start.4
  1743.2 3.7 copy-start.1
where the time goes:
time: 1770 us; the launch traced here: 1750 us
  matrix products  873 us (49%)
  local copies, waits for them, and re-layouts  260 us (15%)
  blocking collectives  232 us (13%)
  waiting for transfers between devices  160 us (9%)
  loops' own time  105 us (6%)
  starting transfers between devices  92.7 us (5%)
  other arithmetic  18.4 us (1%)
    dot_general x24, matrix products, frame_pass(): jnp.dot(row_map.T, right, precision=highest, preferred_element_type=jnp.f...  244 us
    dot_general x24, matrix products, frame_pass(): jnp.dot(row_map, window, precision=highest, preferred_element_type=jnp.fl...  240 us
    dot_general x24, matrix products, frame_pass(): jnp.dot(jnp.dot(row_map, window, precision=highest, preferred_element_typ...  205 us
    dot_general x24, matrix products, frame_pass(): jnp.dot(mismatch, col_map, precision=highest, preferred_element_type=jnp....  184 us
    dynamic_update_slice x24, local copies, waits for them, and re-layouts, accumulate(): lax.dynamic_update_slice_in_dim(total, current + contrib, start, 1)  167 us
    psum x2, blocking collectives, squares(): return lax.psum(jnp.sum(vector * vector), ('wide', 'narrow'))  155 us
    ppermute x18, waiting for transfers between devices, with_halo(): after = lax.ppermute(leading, axis, down)  112 us
    another operation x3, loops' own time, normal_pass(): lax.scan(accumulate, jnp.zeros((extent, 3 * extent), jnp.float32), (obser...  105 us
  transfers between devices with their start and end apart: 36, of which 30 were waited for; matrix products, arithmetic and copies ran while one was open for 0% of the time, Pallas kernels for 0%

commit v1 on v0

v1 whole, which is shorter than its diff:
```python
import functools

import jax
import jax.numpy as jnp
import numpy as np
from jax import lax
from jax.experimental import pallas as pl
from jax.experimental.pallas import tpu as pltpu
from jax.sharding import PartitionSpec as P

NSHIFT = 16
DAMP = 0.05
TS = 512
FS = 128
ROWS = TS + 16
TILES = ROWS // 8
GROUP = 11
PACK = GROUP * 8
F32 = jnp.float32
BF16 = jnp.bfloat16
HIGHEST = lax.Precision.HIGHEST


def tables():
    fraction = np.arange(NSHIFT, dtype=np.float64) / NSHIFT
    offsets = np.arange(8, dtype=np.float64)[None, :] - 3.0 - fraction[:, None]
    lanczos = np.sinc(offsets) * np.sinc(offsets / 4.0)
    lanczos = lanczos / lanczos.sum(axis=1, keepdims=True)
    spread = np.arange(11)[None, :] - np.arange(8)[:, None]
    taps = lanczos @ np.where((spread >= 0) & (spread < 4), 0.25, 0.0)
    out = np.zeros((3, 128, 128), np.float64)
    for feature in range(8):
        weight = feature + 4 if feature < 4 else feature - 4
        for r in range(16):
            for second in range(2):
                if 0 <= r - 4 * second <= 10:
                    out[second, feature * 16 + r, :NSHIFT] = taps[:, r - 4 * second]
            out[2, feature * 16 + r, :NSHIFT] = lanczos[:, weight] * 0.25
    return out.astype(np.float32)


def halves(x):
    high = x.astype(BF16)
    return high, (x - high.astype(F32)).astype(BF16)


def dot(a, b):
    return jnp.dot(a, b, preferred_element_type=F32)


def dot_nt(a, b, precision=None):
    return lax.dot_general(a, b, (((1,), (1,)), ((), ())), precision=precision, preferred_element_type=F32)


def total_of(x):
    return jnp.broadcast_to(jnp.sum(x, axis=(0, 1), keepdims=True), (8, 128))


def kernel(
    n_wide, n_narrow,
    frames, anchor, shift, guess, table,
    r_out, w_out, z_out, coef,
    vec, feat, acc, frb, perm, lhs, lhsb,
    from_side, from_row, from_corner, sums_a, sums_b,
    send, recv, fsend, frecv, floc, asend, arecv, bsend, brecv,
):
    column = lax.axis_index("wide")
    row = lax.axis_index("narrow")
    left, right = lax.rem(column + n_wide - 1, n_wide), lax.rem(column + 1, n_wide)
    up, down = lax.rem(row + n_narrow - 1, n_narrow), lax.rem(row + 1, n_narrow)
    core, chip = lax.rem(column, 2), column // 2
    n_chip = n_wide // 2

    def at(w, n):
        return {"wide": w, "narrow": n}

    near = [at(right, row), at(left, row), at(column, down), at(column, up),
            at(right, down), at(left, down), at(right, up), at(left, up)]
    mates_a = [(row + (k // 2), core + (k % 2)) for k in range(1, 2 * n_narrow)]
    mates_a = [at(chip * 2 + lax.rem(c, 2), lax.rem(r, n_narrow)) for r, c in mates_a]
    mates_b = [at(lax.rem(chip + k, n_chip) * 2 + core, row) for k in range(1, n_chip)]

    barrier = pltpu.get_barrier_semaphore()
    everyone = near + mates_a + mates_b
    for device in everyone:
        pl.semaphore_signal(barrier, inc=1, device_id=device, device_id_type=pl.DeviceIdType.MESH)

    own = pltpu.make_async_copy(frames, frb.at[8 * FS : 16 * FS], floc)
    own.start()

    lane = lax.broadcasted_iota(jnp.int32, (8, 128), 1)
    first, last = lane == 0, lane == 127
    edge = first | last

    k_id = lax.broadcasted_iota(jnp.int32, (512, 512), 0)
    n_id = lax.broadcasted_iota(jnp.int32, (512, 512), 1)
    perm[0] = jnp.where(n_id == 128 * lax.rem(k_id, 4) + k_id // 4, 1.0, 0.0).astype(BF16)
    perm[1] = jnp.where(n_id == 4 * lax.rem(k_id, 128) + k_id // 128, 1.0, 0.0).astype(BF16)

    def pack_tile(v, tile, group, inner, sides):
        packed = None
        for q in range(4):
            for part, offset in sides(q):
                term = pltpu.roll(jnp.where(edge, part, 0.0), 4 * q + offset, axis=1)
                packed = term if packed is None else packed + term
        packed = pltpu.roll(packed, 16 * group, axis=1)
        spot = pl.ds(pl.multiple_of(inner * 8, 8), 8)
        vec[v, 4, spot, :] = vec[v, 4, spot, :] + packed

    def place(tile):
        group = tile // GROUP
        return group, tile - group * GROUP

    zero8 = jnp.zeros((8, 128), F32)

    for q in range(4):
        vec[0, q, 0:8, :] = zero8
        vec[0, q, ROWS - 8 : ROWS, :] = zero8
    for v in range(4):
        vec[v, 4] = jnp.zeros((ROWS, 128), F32)

    def spread_guess(b, carry):
        rows = pl.ds(pl.multiple_of(b * 128, 128), 128)
        high, low = halves(guess[rows, :])
        x = dot(high, perm[0]) + dot(low, perm[0])
        for q in range(4):
            vec[0, q, pl.ds(pl.multiple_of(b * 128 + 8, 8), 128), :] = x[:, q * 128 : q * 128 + 128]
        return carry

    lax.fori_loop(0, 4, spread_guess, 0)

    def pack_guess(i, carry):
        for u in range(4):
            tile = 1 + i * 4 + u
            group, inner = place(tile)
            rows = pl.ds(pl.multiple_of(tile * 8, 8), 8)
            pack_tile(0, tile, group, inner, lambda q: ((vec[0, q, rows, :], 1),))
        return carry

    lax.fori_loop(0, 16, pack_guess, 0)
    vec[0, 4, 512:528, :] = vec[0, 4, 72:88, :]

    pl.semaphore_wait(barrier, len(everyone))

    def exchange(v):
        edges = vec.at[v, 4]
        parts = [
            (edges.at[0:PACK], from_side.at[v, 0]),
            (edges.at[0:PACK], from_side.at[v, 1]),
            (vec.at[v, :, 512:528], from_row.at[v, 0]),
            (vec.at[v, :, 0:16], from_row.at[v, 1]),
            (edges.at[72:88], from_corner.at[v, 0]),
            (edges.at[72:88], from_corner.at[v, 1]),
            (edges.at[0:16], from_corner.at[v, 2]),
            (edges.at[0:16], from_corner.at[v, 3]),
        ]
        copies = []
        for k, (source, target) in enumerate(parts):
            copy = pltpu.make_async_remote_copy(
                src_ref=source, dst_ref=target, send_sem=send.at[v, k], recv_sem=recv.at[v, k],
                device_id=near[k], device_id_type=pl.DeviceIdType.MESH)
            copy.start()
            copies.append(copy)
        return copies

    def settle(v, copies):
        for copy in copies:
            copy.wait()
        has_left, has_right = column > 0, column < n_wide - 1
        has_up, has_down = row > 0, row < n_narrow - 1
        lane16 = lax.broadcasted_iota(jnp.int32, (16, 128), 1)
        sub16 = lax.broadcasted_iota(jnp.int32, (16, 128), 0)
        in_top, in_low = lane16 < 16, (lane16 >= 80) & (lane16 < 96)

        def with_rows(middle, above, below):
            above = jnp.where(in_top & has_up, pltpu.roll(above, 48, axis=1), 0.0)
            below = jnp.where(in_low & has_down, pltpu.roll(below, 80, axis=1), 0.0)
            return jnp.concatenate([middle[0:16] + above, middle[16:72], middle[72:88] + below], axis=0)

        mine = with_rows(vec[v, 4, 0:PACK, :], from_row[v, 0, 4], from_row[v, 1, 4])
        lefts = with_rows(from_side[v, 0], from_corner[v, 0], from_corner[v, 2])
        rights = with_rows(from_side[v, 1], from_corner[v, 1], from_corner[v, 3])
        kind = lax.rem(lax.broadcasted_iota(jnp.int32, (PACK, 128), 1), 4)
        other = jnp.where(kind == 1, pltpu.roll(lefts, 127, axis=1), 0.0)
        other = jnp.where(kind == 3, pltpu.roll(lefts, 3, axis=1), other)
        other = jnp.where(((kind == 1) | (kind == 3)) & has_left, other, 0.0)
        facing = jnp.where(kind == 0, pltpu.roll(rights, 125, axis=1), 0.0)
        facing = jnp.where(kind == 2, pltpu.roll(rights, 1, axis=1), facing)
        facing = jnp.where(((kind == 0) | (kind == 2)) & has_right, facing, 0.0)
        both = mine + other + facing
        both = jnp.where((kind == 3) & (column == 0), 0.0, both)
        both = jnp.where((kind == 2) & (column == n_wide - 1), 0.0, both)
        top = jnp.where(in_top & (sub16 < 8) & (row == 0), 0.0, both[0:16])
        low = jnp.where(in_low & (sub16 >= 8) & (row == n_narrow - 1), 0.0, both[72:88])
        vec[v, 4, 0:PACK, :] = jnp.concatenate([top, both[16:72], low], axis=0)
        for q in range(4):
            x = vec[v, q, 0:16, :] + jnp.where(has_up, from_row[v, 0, q], 0.0)
            vec[v, q, 0:16, :] = jnp.where((sub16 < 8) & (row == 0), 0.0, x)
            x = vec[v, q, 512:528, :] + jnp.where(has_down, from_row[v, 1, q], 0.0)
            vec[v, q, 512:528, :] = jnp.where((sub16 >= 8) & (row == n_narrow - 1), 0.0, x)

    moves = exchange(0)
    frame_moves = []
    for k, device in enumerate((at(right, row), at(left, row))):
        copy = pltpu.make_async_remote_copy(
            src_ref=frames, dst_ref=frb.at[16 * FS * k : 16 * FS * k + 8 * FS], send_sem=fsend.at[k],
            recv_sem=frecv.at[k], device_id=device, device_id_type=pl.DeviceIdType.MESH)
        copy.start()
        frame_moves.append(copy)

    n_frames = 8 * n_wide
    f_id = lax.broadcasted_iota(jnp.int32, (n_frames, 128), 0)
    slot = lax.broadcasted_iota(jnp.int32, (n_frames, 128), 1)
    slot = slot - (slot // 32) * 32
    wanted = lax.rem(slot + 8 * left, n_frames)
    pick = jnp.where((f_id == wanted) & (slot < 24), 1.0, 0.0).astype(BF16)
    looks = jnp.where(jnp.broadcast_to(anchor[...], (16, n_frames)) == column, 1.0, 0.0).astype(BF16)
    used = dot(looks, pick)[0:1]
    codes = [shift[0, pl.ds(pl.multiple_of(8 * o, 8), 8), :] for o in (left, column, right)]
    codes = jnp.concatenate((codes + [jnp.zeros((8, 2), jnp.int32)]) * 4, axis=0)
    lane128 = lax.broadcasted_iota(jnp.int32, (128, 128), 1)
    one_a = jnp.where(codes[:, 0:1] == lane128, 1.0, 0.0)
    one_b = jnp.where(codes[:, 1:2] == lane128, 1.0, 0.0)
    second = lax.rem(lane128 // 32, 2) == 1
    tall = dot_nt(table[2], one_b, HIGHEST) * jnp.where(
        second, dot_nt(table[1], one_a, HIGHEST), dot_nt(table[0], one_a, HIGHEST)) * used
    for which, keep in enumerate((second, lane128 >= 0, jnp.logical_not(second))):
        kept = jnp.where(keep, tall, 0.0)
        high, low = halves(kept)
        lhsb[which, :, 0:128] = high
        lhsb[which, :, 128:256] = jnp.where(lane128 < 64, low.astype(F32), 0.0).astype(BF16)
        half = jnp.where(lane128 < 64, kept, 0.0)
        high, low = halves(dot_nt(half, half, HIGHEST))
        lhs[which, :, 0:128] = high
        lhs[which, :, 128:256] = high
        lhs[which, :, 256:384] = low

    settle(0, moves)

    def unfold(v):
        def tile_step(tile):
            group, inner = place(tile)
            rows = pl.ds(pl.multiple_of(tile * 8, 8), 8)
            packed = vec[v, 4, pl.ds(pl.multiple_of(inner * 8, 8), 8), :]
            packed = pltpu.roll(packed, 127 - 16 * group, axis=1)
            mid, nxt, prv = [], [], []
            for q in range(4):
                spun = packed if q == 0 else pltpu.roll(packed, 128 - 4 * q, axis=1)
                x = jnp.where(edge, spun, vec[v, q, rows, :])
                vec[v, q, rows, :] = x
                side = pltpu.roll(packed, 126 - 4 * q, axis=1)
                mid.append(x)
                prv.append(jnp.where(first, side, pltpu.roll(x, 1, axis=1)))
                if q < 3:
                    nxt.append(jnp.where(last, side, pltpu.roll(x, 127, axis=1)))
            m23, p23 = mid[2] + mid[3], prv[2] + prv[3]
            m123, p123 = mid[1] + m23, prv[1] + p23
            m01, n01 = mid[0] + mid[1], nxt[0] + nxt[1]
            out = [mid[0] + m123, m123 + nxt[0], m23 + n01, mid[3] + (n01 + nxt[2]),
                   prv[0] + p123, p123 + mid[0], p23 + m01, prv[3] + (m01 + mid[2])]
            for f in range(8):
                feat[f, rows, :] = out[f]

        def step(i, carry):
            for u in range(3):
                tile_step(i * 3 + u)
            return carry

        lax.fori_loop(0, TILES // 3, step, 0)

    def blocks(starts):
        highs, lows = [], []
        for start in starts:
            pairs = [halves(feat[f, pl.ds(start, 16), :]) for f in range(8)]
            highs.append(jnp.concatenate([p[0] for p in pairs], axis=0))
            lows.append(jnp.concatenate([p[1] for p in pairs], axis=0))
        high = highs[0] if len(starts) == 1 else jnp.concatenate(highs, axis=1)
        low = lows[0] if len(starts) == 1 else jnp.concatenate(lows, axis=1)
        return jnp.concatenate([high, low, high], axis=0)

    def mix():
        out = dot(lhs[0], blocks([0]))
        for f in range(8):
            acc[f, 0:8, :] = out[16 * f : 16 * f + 8]
        carry = tuple(out[16 * f + 8 : 16 * f + 16] for f in range(8))

        def pair(i, carry):
            start = pl.multiple_of(8 + i * 16, 8)
            out = dot(lhs[1], blocks([start, start + 8]))
            later = []
            for f in range(8):
                acc[f, pl.ds(start, 8), :] = carry[f] + out[16 * f : 16 * f + 8, 0:128]
                acc[f, pl.ds(start + 8, 8), :] = (
                    out[16 * f + 8 : 16 * f + 16, 0:128] + out[16 * f : 16 * f + 8, 128:256])
                later.append(out[16 * f + 8 : 16 * f + 16, 128:256])
            return tuple(later)

        carry = lax.fori_loop(0, 31, pair, carry)
        for start, which in ((504, 1), (512, 2)):
            out = dot(lhs[which], blocks([start]))
            for f in range(8):
                acc[f, start : start + 8, :] = carry[f] + out[16 * f : 16 * f + 8]
            carry = tuple(out[16 * f + 8 : 16 * f + 16] for f in range(8))
        for f in range(8):
            acc[f, 520:528, :] = carry[f]

    def take_frames():
        def block(start, before, after, which):
            parts = []
            for i in (before, after):
                parts.append(frb[pl.ds(i, 24, stride=FS), :])
                parts.append(zero8)
            high, low = halves(jnp.concatenate(parts, axis=0))
            both = jnp.concatenate([high, low], axis=0)
            out = dot(lhsb[which, :, 0:128], both) + dot(lhsb[which, :, 128:256], both)
            for f in range(8):
                acc[f, pl.ds(start, 16), :] = acc[f, pl.ds(start, 16), :] - out[16 * f : 16 * f + 16]

        block(0, 0, 0, 0)

        def step(i, carry):
            for u in range(3):
                a = 1 + i * 3 + u
                block(pl.multiple_of(8 * a, 8), 2 * a - 1, 2 * a, 1)
            return carry

        lax.fori_loop(0, 21, step, 0)
        block(512, 127, 127, 2)

    def fold(v, sign, measure):
        def tile_step(tile, inside, sums):
            group, inner = place(tile)
            rows = pl.ds(pl.multiple_of(tile * 8, 8), 8)
            cur = [acc[q, rows, :] for q in range(4)]
            pre = [acc[4 + q, rows, :] for q in range(4)]
            rolled = [pltpu.roll(x, 127, axis=1) for x in pre]
            here = [c + jnp.where(last, 0.0, p) for c, p in zip(cur, rolled)]
            back = [p + jnp.where(last, 0.0, c) for c, p in zip(cur, rolled)]
            h01 = here[0] + here[1]
            h012 = h01 + here[2]
            k23 = back[2] + back[3]
            out = [here[0] + pltpu.roll(back[1] + k23, 1, axis=1), h01 + pltpu.roll(k23, 1, axis=1),
                   h012 + pltpu.roll(back[3], 1, axis=1), h012 + here[3]]
            h23 = here[2] + here[3]
            r01 = pre[0] + pre[1]
            r012 = r01 + pre[2]
            over = [jnp.where(first, pre[0], here[1] + h23), jnp.where(first, r01, h23),
                    jnp.where(first, r012, here[3]), jnp.where(first, r012 + pre[3], 0.0)]
            old = [vec[v, q, rows, :] for q in range(4)]
            if inside:
                out = [o + DAMP * x for o, x in zip(out, old)]
            if sign < 0:
                out, over = [-o for o in out], [-o for o in over]
            for q in range(4):
                vec[v + 1, q, rows, :] = out[q]
            pack_tile(v + 1, tile, group, inner, lambda q: ((out[q], 1), (over[q], 3)))
            return measure(rows, inside, old, out, sums)

        def step(i, sums):
            for u in range(4):
                sums = tile_step(1 + i * 4 + u, True, sums)
            return sums

        sums = tile_step(0, False, (zero8, zero8, zero8))
        sums = lax.fori_loop(0, 16, step, sums)
        sums = tile_step(TILES - 1, False, sums)
        vec[v + 1, 4, 512:528, :] = vec[v + 1, 4, 72:88, :]
        return sums

    def outer_columns(product):
        kind = lax.rem(lax.broadcasted_iota(jnp.int32, (PACK, 128), 1), 4)
        product = jnp.where(kind >= 2, product, 0.0)
        while product.shape[0] > 8:
            product = product[0:8] + product[8:] if product.shape[0] == 16 else jnp.concatenate(
                [product[0:8] + product[8:16], product[16:]], axis=0)
        return product

    def gather_a(call, values):
        for i, value in enumerate(values):
            sums_a[call, 0, i] = value
        copies = []
        for k, device in enumerate(mates_a):
            copy = pltpu.make_async_remote_copy(
                src_ref=sums_a.at[call, 0], dst_ref=sums_a.at[call, k + 1], send_sem=asend.at[call, k],
                recv_sem=arecv.at[call, k], device_id=device, device_id_type=pl.DeviceIdType.MESH)
            copy.start()
            copies.append(copy)
        return copies

    def gather_b(call, copies):
        for copy in copies:
            copy.wait()
        for i in range(3):
            value = sums_a[call, 0, i]
            for k in range(len(mates_a)):
                value = value + sums_a[call, k + 1, i]
            sums_b[call, 0, i] = value
        copies = []
        for k, device in enumerate(mates_b):
            copy = pltpu.make_async_remote_copy(
                src_ref=sums_b.at[call, 0], dst_ref=sums_b.at[call, k + 1], send_sem=bsend.at[call, k],
                recv_sem=brecv.at[call, k], device_id=device, device_id_type=pl.DeviceIdType.MESH)
            copy.start()
            copies.append(copy)
        return copies

    def finish_sums(call, copies):
        for copy in copies:
            copy.wait()
        values = []
        for i in range(3):
            value = sums_b[call, 0, i]
            for k in range(len(mates_b)):
                value = value + sums_b[call, k + 1, i]
            values.append(total_of(value))
        return values

    def write_pixels(v, out):
        def step(b, carry):
            rows = pl.ds(pl.multiple_of(b * 128 + 8, 8), 128)
            x = jnp.concatenate([vec[v, q, rows, :] for q in range(4)], axis=1)
            high, low = halves(x)
            out[pl.ds(pl.multiple_of(b * 128, 128), 128), :] = dot(high, perm[1]) + dot(low, perm[1])
            return carry

        lax.fori_loop(0, 4, step, 0)

    def patch_edges(v):
        def step(i, carry):
            for u in range(4):
                tile = 1 + i * 4 + u
                group, inner = place(tile)
                rows = pl.ds(pl.multiple_of(tile * 8, 8), 8)
                packed = vec[v, 4, pl.ds(pl.multiple_of(inner * 8, 8), 8), :]
                packed = pltpu.roll(packed, 127 - 16 * group, axis=1)
                for q in range(4):
                    spun = packed if q == 0 else pltpu.roll(packed, 128 - 4 * q, axis=1)
                    vec[v, q, rows, :] = jnp.where(edge, spun, vec[v, q, rows, :])
            return carry

        lax.fori_loop(0, 16, step, 0)

    unfold(0)
    mix()
    own.wait()
    for copy in frame_moves:
        copy.wait()
    take_frames()
    fold(0, -1.0, lambda rows, inside, old, out, sums: sums)
    settle(1, exchange(1))

    unfold(1)
    mix()

    def measure_w(rows, inside, old, out, sums):
        rr, rw, _ = sums
        for q in range(4):
            rw = rw + old[q] * out[q]
            if inside:
                rr = rr + old[q] * old[q]
        return rr, rw, zero8

    rr, rw, _ = fold(1, 1.0, measure_w)
    rw = rw + outer_columns(vec[1, 4, 0:PACK, :] * vec[2, 4, 0:PACK, :])
    moves = exchange(2)
    first_sums = gather_a(0, (rr, rw, zero8))
    write_pixels(1, r_out)
    settle(2, moves)
    first_sums = gather_b(0, first_sums)

    unfold(2)
    mix()
    rr, rw, _ = finish_sums(0, first_sums)
    alpha = rr / rw

    def measure_z(rows, inside, old, out, sums):
        ss, sw, sz = sums
        for q in range(4):
            s = vec[1, q, rows, :] - alpha * old[q]
            sz = sz + s * out[q]
            if inside:
                ss = ss + s * s
                sw = sw + s * old[q]
        return ss, sw, sz

    ss, sw, sz = fold(2, 1.0, measure_z)
    s_edge = vec[1, 4, 0:PACK, :] - alpha[0:1, :] * vec[2, 4, 0:PACK, :]
    sz = sz + outer_columns(s_edge * vec[3, 4, 0:PACK, :])
    last_sums = gather_a(1, (ss, sw, sz))
    moves = exchange(3)
    write_pixels(2, w_out)
    last_sums = gather_b(1, last_sums)
    settle(3, moves)
    patch_edges(3)
    write_pixels(3, z_out)
    ss, sw, sz = finish_sums(1, last_sums)
    beta = ss / rr
    curve = (sw - alpha * sz) + 2.0 * beta * sw + beta * beta * rw
    step = ss / curve
    coef[0] = alpha + step * (1.0 + beta)
    coef[1] = step * alpha


def on_device(n_wide, n_narrow, frames, anchor, shift, guess):
    vmem = pl.BlockSpec(memory_space=pltpu.VMEM)
    image = jax.ShapeDtypeStruct((TS, TS), F32)
    dma = pltpu.SemaphoreType.DMA
    n_a, n_b = 2 * n_narrow, n_wide // 2
    r, w, z, coef = pl.pallas_call(
        functools.partial(kernel, n_wide, n_narrow),
        out_shape=(image, image, image, jax.ShapeDtypeStruct((2, 8, 128), F32)),
        in_specs=[pl.BlockSpec(memory_space=pl.ANY), vmem, vmem, vmem, vmem],
        out_specs=(vmem, vmem, vmem, vmem),
        scratch_shapes=[
            pltpu.VMEM((4, 5, ROWS, 128), F32),
            pltpu.VMEM((8, ROWS, 128), F32),
            pltpu.VMEM((8, ROWS, 128), F32),
            pltpu.VMEM((24 * FS, 128), F32),
            pltpu.VMEM((2, 512, 512), BF16),
            pltpu.VMEM((3, 128, 384), BF16),
            pltpu.VMEM((3, 128, 256), BF16),
            pltpu.VMEM((4, 2, PACK, 128), F32),
            pltpu.VMEM((4, 2, 5, 16, 128), F32),
            pltpu.VMEM((4, 4, 16, 128), F32),
            pltpu.VMEM((2, n_a, 3, 8, 128), F32),
            pltpu.VMEM((2, n_b, 3, 8, 128), F32),
            dma((4, 8)), dma((4, 8)), dma((2,)), dma((2,)), dma,
            dma((2, n_a)), dma((2, n_a)), dma((2, n_b)), dma((2, n_b)),
        ],
        compiler_params=pltpu.CompilerParams(
            collective_id=0, has_side_effects=True, vmem_limit_bytes=48 * 2**20),
    )(frames.reshape(8 * FS, FS), anchor, shift, guess, jnp.asarray(tables()))
    c1, c2 = coef[0, 0, 0], coef[1, 0, 0]
    return guess + c1 * r - c2 * w, r - c1 * w + c2 * z


def solution(mesh):
    placed = (P("narrow", "wide", None, None), P("narrow", None), P("narrow", None, None), P("narrow", "wide"))
    return jax.shard_map(
        functools.partial(on_device, mesh.shape["wide"], mesh.shape["narrow"]),
        mesh=mesh,
        in_specs=placed,
        out_specs=(P("narrow", "wide"), P("narrow", "wide")),
        check_vma=False,
    )
```

time: 1770 us -> 151 us (0.09); the launches traced: 1750 us -> 151 us
  matrix products: 873 us -> 0 us
  local copies, waits for them, and re-layouts: 260 us -> 4.6 us
  blocking collectives: 232 us -> 0 us
  waiting for transfers between devices: 160 us -> 0 us
  Pallas kernels: 0 us -> 143 us
  loops' own time: 105 us -> 0 us
  starting transfers between devices: 92.7 us -> 0 us
    dot_general x97 -> x0, matrix products: 873 us -> none  [the longest x24 244 us: frame_pass(): jnp.dot(row_map.T, right, precision=highest, preferred_element_type=jnp.f...]
    psum x3 -> x0, blocking collectives: 232 us -> none  [the longest x2 155 us: squares(): return lax.psum(jnp.sum(vector * vector), ('wide', 'narrow'))]
    dynamic_update_slice x24 -> x0, local copies, waits for them, and re-layouts: 167 us -> none  [accumulate(): lax.dynamic_update_slice_in_dim(total, current + contrib, start, 1)]
    ppermute x36 -> x0, waiting for transfers between devices: 160 us -> none  [the longest x18 112 us: with_halo(): after = lax.ppermute(leading, axis, down)]
    pallas_call x0 -> x1, Pallas kernels: none -> 143 us  [on_device(): pl.pallas_call(functools.partial(kernel, n_wide, n_narrow), out_shape=(im...]
    another operation x3 -> x0, loops' own time: 105 us -> none  [normal_pass(): lax.scan(accumulate, jnp.zeros((extent, 3 * extent), jnp.float32), (obser...]
    ppermute x36 -> x0, starting transfers between devices: 92.7 us -> none  [the longest x18 60.4 us: with_halo(): before = lax.ppermute(last, axis, up)]
    slice x84 -> x1, local copies, waits for them, and re-layouts: 55.5 us -> 0.6 us  [on_device(): c1, c2 = (coef[0, 0, 0], coef[1, 0, 0])]
  transfers between devices with their start and end apart: 36 -> 0, of which waited for: 30 -> 0; matrix products, arithmetic and copies ran while one was open for 0% -> 0% of each run, Pallas kernels for 0% -> 0%
where the time goes in v1:
time: 151 us
  Pallas kernels  143 us (95%)
  local copies, waits for them, and re-layouts  4.6 us (3%)
  other arithmetic  3.07 us (2%)
    pallas_call x1, Pallas kernels, on_device(): pl.pallas_call(functools.partial(kernel, n_wide, n_narrow), out_shape=(im...  143 us
    unnamed x9, local copies, waits for them, and re-layouts  4.01 us
    add x1, other arithmetic, on_device(): return (guess + c1 * r - c2 * w, r - c1 * w + c2 * z)  3.07 us

profile of v1, /device:TPU:1, one launch (start us, length us, event | category | flops | bytes accessed | tf_op | source)
XLA Modules:
  0.0 151.1 jit_solution(11271968051426415521)
XLA Ops:
  0.6 0.0 copy-start.3
  0.6 0.8 copy.7.shift
  1.5 0.0 copy-done.3
  1.5 0.0 copy-start
  1.5 1.2 copy-done
  2.7 0.0 copy-start.1
  2.7 1.0 copy-done.1
  3.7 0.0 copy-start.2
  3.7 0.9 copy-done.2
  4.7 142.7 %shard_map.68 = (f32[512,512]{1,0:T(8,128)S(1)}, f32[512,512]{1,0:T(8,128)S(1)}, f32[512,512]{1,0:T(8,128)S(1)}, f32[2,8,128]{2,1,0:T(8,128)S(1)}) custom-call(f32[1024,128]{1,0:T(8,128)S(1)} %bitcast.3, s32[1,256]{1,0:T(1,128)S(1)} %copy-done.3, s32[1,256,2]{2,1,0:T(8,128)S(1)} %copy.7.shift, f32[512,512]{1,0:T(8,128)S(1)} %copy-done, ...), custom_call_target="tpu_custom_call" | custom-call | tf_op jit(solution)/shard_map/pallas_call | solution.py:509
  147.4 0.6 fusion
  148.0 3.1 %multiply_add_fusion = (f32[512,512]{1,0:T(8,128)}, f32[512,512]{1,0:T(8,128)}) fusion(f32[512,512]{1,0:T(8,128)S(1)} %get-tuple-element.9, f32[512,512]{1,0:T(8,128)S(1)} %get-tuple-element.7, f32[512,512]{1,0:T(8,128)S(1)} %get-tuple-element.8, f32[]{:T(128)} %bitcast.2, f32[]{:T(128)} %bitcast.1, f32[512,512]{1,0:T(8,128)S(1)} %copy-done), kind=kLoop, calls=%fused_computation | loop fusion | flops 2097152 | bytes 6291464 | tf_op jit(solution)/shard_map/add | solution.py:534
Async XLA Ops:
  0.6 0.8 copy-start.3
  1.5 1.2 copy-start
  2.7 1.0 copy-start.1
  3.7 0.9 copy-start.2

commit v2 on v1

--- a/solution.py
+++ b/solution.py
@@ -18,6 +18,9 @@
 PACK = GROUP * 8
 F32 = jnp.float32
 BF16 = jnp.bfloat16
+UNFOLD = 264
+FOLD = 264
+MIX = 32
 HIGHEST = lax.Precision.HIGHEST
 
 
@@ -60,7 +63,7 @@
     n_wide, n_narrow,
     frames, anchor, shift, guess, table,
     r_out, w_out, z_out, coef,
-    vec, feat, acc, frb, perm, lhs, lhsb,
+    vec, whole, wide_edges, feat, acc, more, frb, perm, lhs, lhsb,
     from_side, from_row, from_corner, sums_a, sums_b,
     send, recv, fsend, frecv, floc, asend, arecv, bsend, brecv,
 ):
@@ -88,57 +91,56 @@
     own = pltpu.make_async_copy(frames, frb.at[8 * FS : 16 * FS], floc)
     own.start()
 
-    lane = lax.broadcasted_iota(jnp.int32, (8, 128), 1)
-    first, last = lane == 0, lane == 127
-    edge = first | last
-
-    k_id = lax.broadcasted_iota(jnp.int32, (512, 512), 0)
-    n_id = lax.broadcasted_iota(jnp.int32, (512, 512), 1)
-    perm[0] = jnp.where(n_id == 128 * lax.rem(k_id, 4) + k_id // 4, 1.0, 0.0).astype(BF16)
-    perm[1] = jnp.where(n_id == 4 * lax.rem(k_id, 128) + k_id // 128, 1.0, 0.0).astype(BF16)
-
-    def pack_tile(v, tile, group, inner, sides):
+    k_id = lax.broadcasted_iota(jnp.int32, (512, 128), 0)
+    n_id = lax.broadcasted_iota(jnp.int32, (512, 128), 1)
+    for which, target in enumerate((128 * (k_id & 3) + (k_id >> 2), 4 * (k_id & 127) + (k_id >> 7))):
+        for c in range(4):
+            perm[which, :, c * 128 : c * 128 + 128] = jnp.where(n_id + 128 * c == target, 1.0, 0.0).astype(BF16)
+
+    zero8 = jnp.zeros((8, 128), F32)
+
+    def edge_masks(size):
+        lane = lax.broadcasted_iota(jnp.int32, (size, 128), 1)
+        return lane == 0, lane == 127
+
+    def gather_edges(sides):
         packed = None
-        for q in range(4):
-            for part, offset in sides(q):
-                term = pltpu.roll(jnp.where(edge, part, 0.0), 4 * q + offset, axis=1)
-                packed = term if packed is None else packed + term
-        packed = pltpu.roll(packed, 16 * group, axis=1)
-        spot = pl.ds(pl.multiple_of(inner * 8, 8), 8)
-        vec[v, 4, spot, :] = vec[v, 4, spot, :] + packed
-
-    def place(tile):
-        group = tile // GROUP
-        return group, tile - group * GROUP
-
-    zero8 = jnp.zeros((8, 128), F32)
+        for shift_by, part in sides:
+            first, last = edge_masks(part.shape[0])
+            term = pltpu.roll(jnp.where(first | last, part, 0.0), shift_by, axis=1)
+            packed = term if packed is None else packed + term
+        return packed
+
+    def pack(v):
+        packed = wide_edges[0:PACK, :]
+        for g in range(1, 6):
+            packed = packed + pltpu.roll(wide_edges[g * PACK : g * PACK + PACK, :], 16 * g, axis=1)
+        vec[v, 4, 0:PACK, :] = packed
+        vec[v, 4, 512:528, :] = packed[72:88]
+
+    def unpack(v):
+        for g in range(6):
+            wide_edges[g * PACK : g * PACK + PACK, :] = pltpu.roll(vec[v, 4, 0:PACK, :], 127 - 16 * g, axis=1)
 
     for q in range(4):
         vec[0, q, 0:8, :] = zero8
         vec[0, q, ROWS - 8 : ROWS, :] = zero8
-    for v in range(4):
-        vec[v, 4] = jnp.zeros((ROWS, 128), F32)
+    wide_edges[0:8, :] = zero8
+    wide_edges[ROWS - 8 : ROWS, :] = zero8
 
     def spread_guess(b, carry):
         rows = pl.ds(pl.multiple_of(b * 128, 128), 128)
+        into = pl.ds(pl.multiple_of(b * 128 + 8, 8), 128)
         high, low = halves(guess[rows, :])
         x = dot(high, perm[0]) + dot(low, perm[0])
+        x = [x[:, q * 128 : q * 128 + 128] for q in range(4)]
         for q in range(4):
-            vec[0, q, pl.ds(pl.multiple_of(b * 128 + 8, 8), 128), :] = x[:, q * 128 : q * 128 + 128]
+            vec[0, q, into, :] = x[q]
+        wide_edges[into, :] = gather_edges([(4 * q + 1, x[q]) for q in range(4)])
         return carry
 
     lax.fori_loop(0, 4, spread_guess, 0)
-
-    def pack_guess(i, carry):
-        for u in range(4):
-            tile = 1 + i * 4 + u
-            group, inner = place(tile)
-            rows = pl.ds(pl.multiple_of(tile * 8, 8), 8)
-            pack_tile(0, tile, group, inner, lambda q: ((vec[0, q, rows, :], 1),))
-        return carry
-
-    lax.fori_loop(0, 16, pack_guess, 0)
-    vec[0, 4, 512:528, :] = vec[0, 4, 72:88, :]
+    pack(0)
 
     pl.semaphore_wait(barrier, len(everyone))
 
@@ -237,22 +239,28 @@
 
     settle(0, moves)
 
-    def unfold(v):
-        def tile_step(tile):
-            group, inner = place(tile)
-            rows = pl.ds(pl.multiple_of(tile * 8, 8), 8)
-            packed = vec[v, 4, pl.ds(pl.multiple_of(inner * 8, 8), 8), :]
-            packed = pltpu.roll(packed, 127 - 16 * group, axis=1)
+    def unfold(v, features=True):
+        unpack(v)
+
+        def step(i, carry):
+            rows = pl.ds(pl.multiple_of(i * UNFOLD, 8), UNFOLD)
+            first, last = edge_masks(UNFOLD)
+            packed = wide_edges[rows, :]
+            raw = [vec[v, q, rows, :] for q in range(4)]
             mid, nxt, prv = [], [], []
             for q in range(4):
                 spun = packed if q == 0 else pltpu.roll(packed, 128 - 4 * q, axis=1)
-                x = jnp.where(edge, spun, vec[v, q, rows, :])
-                vec[v, q, rows, :] = x
-                side = pltpu.roll(packed, 126 - 4 * q, axis=1)
+                x = jnp.where(first | last, spun, raw[q])
                 mid.append(x)
-                prv.append(jnp.where(first, side, pltpu.roll(x, 1, axis=1)))
-                if q < 3:
-                    nxt.append(jnp.where(last, side, pltpu.roll(x, 127, axis=1)))
+                if features:
+                    side = pltpu.roll(packed, 126 - 4 * q, axis=1)
+                    prv.append(jnp.where(first, side, pltpu.roll(x, 1, axis=1)))
+                    if q < 3:
+                        nxt.append(jnp.where(last, side, pltpu.roll(x, 127, axis=1)))
+            for q in range(4):
+                whole[v, q, rows, :] = mid[q]
+            if not features:
+                return carry
             m23, p23 = mid[2] + mid[3], prv[2] + prv[3]
             m123, p123 = mid[1] + m23, prv[1] + p23
             m01, n01 = mid[0] + mid[1], nxt[0] + nxt[1]
@@ -260,13 +268,12 @@
                    prv[0] + p123, p123 + mid[0], p23 + m01, prv[3] + (m01 + mid[2])]
             for f in range(8):
                 feat[f, rows, :] = out[f]
-
-        def step(i, carry):
-            for u in range(3):
-                tile_step(i * 3 + u)
             return carry
 
-        lax.fori_loop(0, TILES // 3, step, 0)
+        lax.fori_loop(0, ROWS // UNFOLD, step, 0)
+
+    def join(parts):
+        return parts[0] if len(parts) == 1 else jnp.concatenate(parts, axis=1)
 
     def blocks(starts):
         highs, lows = [], []
@@ -274,65 +281,87 @@
             pairs = [halves(feat[f, pl.ds(start, 16), :]) for f in range(8)]
             highs.append(jnp.concatenate([p[0] for p in pairs], axis=0))
             lows.append(jnp.concatenate([p[1] for p in pairs], axis=0))
-        high = highs[0] if len(starts) == 1 else jnp.concatenate(highs, axis=1)
-        low = lows[0] if len(starts) == 1 else jnp.concatenate(lows, axis=1)
+        high, low = join(highs), join(lows)
         return jnp.concatenate([high, low, high], axis=0)
 
+    def stack(outs, carry):
+        done = []
+        for out in outs:
+            done.append([out[16 * f : 16 * f + 8] if carry is None else carry[f] + out[16 * f : 16 * f + 8]
+                         for f in range(8)])
+            carry = [out[16 * f + 8 : 16 * f + 16] for f in range(8)]
+        return done, carry
+
+    def sweep(results, save):
+        def some(starts, kinds, carry):
+            outs = []
+            for k in range(0, len(starts), 2):
+                outs.extend(results(starts[k : k + 2], kinds[k : k + 2]))
+            done, carry = stack(outs, carry)
+            for start, tiles in zip(starts, done):
+                save(start, tiles)
+            return tuple(carry)
+
+        carry = some([8 * k for k in range(MIX)], [0] + [1] * (MIX - 1), None)
+
+        def step(i, carry):
+            start = pl.multiple_of(i * (8 * MIX), 8)
+            return some([start + 8 * k for k in range(MIX)], [1] * MIX, carry)
+
+        carry = lax.fori_loop(1, 64 // MIX, step, carry)
+        carry = some([512], [2], carry)
+        save(520, carry)
+
+    def cut(out):
+        return [out[:, 128 * k : 128 * k + 128] for k in range(out.shape[1] // 128)]
+
     def mix():
-        out = dot(lhs[0], blocks([0]))
-        for f in range(8):
-            acc[f, 0:8, :] = out[16 * f : 16 * f + 8]
-        carry = tuple(out[16 * f + 8 : 16 * f + 16] for f in range(8))
-
-        def pair(i, carry):
-            start = pl.multiple_of(8 + i * 16, 8)
-            out = dot(lhs[1], blocks([start, start + 8]))
-            later = []
+        def results(starts, kinds):
+            if len(set(kinds)) > 1:
+                return [dot(lhs[w], blocks([s])) for s, w in zip(starts, kinds)]
+            return cut(dot(lhs[kinds[0]], blocks(starts)))
+
+        def save(start, tiles):
             for f in range(8):
-                acc[f, pl.ds(start, 8), :] = carry[f] + out[16 * f : 16 * f + 8, 0:128]
-                acc[f, pl.ds(start + 8, 8), :] = (
-                    out[16 * f + 8 : 16 * f + 16, 0:128] + out[16 * f : 16 * f + 8, 128:256])
-                later.append(out[16 * f + 8 : 16 * f + 16, 128:256])
-            return tuple(later)
-
-        carry = lax.fori_loop(0, 31, pair, carry)
-        for start, which in ((504, 1), (512, 2)):
-            out = dot(lhs[which], blocks([start]))
+                acc[f, pl.ds(start, 8), :] = tiles[f]
+
+        sweep(results, save)
+
+    def take_frames():
+        def pixels(start, kind):
+            sample = start // 4
+            rows = [0 if kind == 0 else sample - 1, FS - 1 if kind == 2 else sample]
+            parts = []
+            for i in rows:
+                parts += [frb[pl.ds(i, 24, stride=FS), :], zero8]
+            high, low = halves(jnp.concatenate(parts, axis=0))
+            return jnp.concatenate([high, low], axis=0)
+
+        def results(starts, kinds):
+            if len(set(kinds)) > 1:
+                return [results([s], [w])[0] for s, w in zip(starts, kinds)]
+            both = join([pixels(s, w) for s, w in zip(starts, kinds)])
+            return cut(dot(lhsb[kinds[0]], jnp.concatenate([both, both], axis=0)))
+
+        def save(start, tiles):
             for f in range(8):
-                acc[f, start : start + 8, :] = carry[f] + out[16 * f : 16 * f + 8]
-            carry = tuple(out[16 * f + 8 : 16 * f + 16] for f in range(8))
-        for f in range(8):
-            acc[f, 520:528, :] = carry[f]
-
-    def take_frames():
-        def block(start, before, after, which):
-            parts = []
-            for i in (before, after):
-                parts.append(frb[pl.ds(i, 24, stride=FS), :])
-                parts.append(zero8)
-            high, low = halves(jnp.concatenate(parts, axis=0))
-            both = jnp.concatenate([high, low], axis=0)
-            out = dot(lhsb[which, :, 0:128], both) + dot(lhsb[which, :, 128:256], both)
-            for f in range(8):
-                acc[f, pl.ds(start, 16), :] = acc[f, pl.ds(start, 16), :] - out[16 * f : 16 * f + 16]
-
-        block(0, 0, 0, 0)
-
-        def step(i, carry):
-            for u in range(3):
-                a = 1 + i * 3 + u
-                block(pl.multiple_of(8 * a, 8), 2 * a - 1, 2 * a, 1)
-            return carry
-
-        lax.fori_loop(0, 21, step, 0)
-        block(512, 127, 127, 2)
-
-    def fold(v, sign, measure):
-        def tile_step(tile, inside, sums):
-            group, inner = place(tile)
-            rows = pl.ds(pl.multiple_of(tile * 8, 8), 8)
+                more[f, pl.ds(start, 8), :] = tiles[f]
+
+        sweep(results, save)
+
+    def fold(v, sign, measure, counts):
+        def step(i, sums):
+            rows = pl.ds(pl.multiple_of(i * FOLD, 8), FOLD)
+            first, last = edge_masks(FOLD)
+            row_id = i * FOLD + lax.broadcasted_iota(jnp.int32, (FOLD, 128), 0)
+            inside = (row_id >= 8) & (row_id < ROWS - 8)
+            damp = jnp.where(inside, DAMP, 0.0)
             cur = [acc[q, rows, :] for q in range(4)]
             pre = [acc[4 + q, rows, :] for q in range(4)]
+            if v == 0:
+                cur = [c - more[q, rows, :] for q, c in enumerate(cur)]
+                pre = [p - more[4 + q, rows, :] for q, p in enumerate(pre)]
+            old = [whole[v, q, rows, :] for q in range(4)]
             rolled = [pltpu.roll(x, 127, axis=1) for x in pre]
             here = [c + jnp.where(last, 0.0, p) for c, p in zip(cur, rolled)]
             back = [p + jnp.where(last, 0.0, c) for c, p in zip(cur, rolled)]
@@ -346,34 +375,29 @@
             r012 = r01 + pre[2]
             over = [jnp.where(first, pre[0], here[1] + h23), jnp.where(first, r01, h23),
                     jnp.where(first, r012, here[3]), jnp.where(first, r012 + pre[3], 0.0)]
-            old = [vec[v, q, rows, :] for q in range(4)]
-            if inside:
-                out = [o + DAMP * x for o, x in zip(out, old)]
+            out = [o + damp * x for o, x in zip(out, old)]
             if sign < 0:
                 out, over = [-o for o in out], [-o for o in over]
+            packed = gather_edges([(4 * q + 1, out[q]) for q in range(4)] + [(4 * q + 3, over[q]) for q in range(4)])
+            more_sums = measure(rows, inside, old, out)
             for q in range(4):
                 vec[v + 1, q, rows, :] = out[q]
-            pack_tile(v + 1, tile, group, inner, lambda q: ((out[q], 1), (over[q], 3)))
-            return measure(rows, inside, old, out, sums)
-
-        def step(i, sums):
-            for u in range(4):
-                sums = tile_step(1 + i * 4 + u, True, sums)
-            return sums
-
-        sums = tile_step(0, False, (zero8, zero8, zero8))
-        sums = lax.fori_loop(0, 16, step, sums)
-        sums = tile_step(TILES - 1, False, sums)
-        vec[v + 1, 4, 512:528, :] = vec[v + 1, 4, 72:88, :]
-        return sums
+            wide_edges[rows, :] = packed
+            return tuple(s + m for s, m in zip(sums, more_sums))
+
+        sums = lax.fori_loop(0, ROWS // FOLD, step, (jnp.zeros((FOLD, 128), F32),) * counts)
+        pack(v + 1)
+        return [fewer_rows(s) for s in sums]
+
+    def fewer_rows(x):
+        total = x[0:8]
+        for k in range(8, x.shape[0], 8):
+            total = total + x[k : k + 8]
+        return total
 
     def outer_columns(product):
-        kind = lax.rem(lax.broadcasted_iota(jnp.int32, (PACK, 128), 1), 4)
-        product = jnp.where(kind >= 2, product, 0.0)
-        while product.shape[0] > 8:
-            product = product[0:8] + product[8:] if product.shape[0] == 16 else jnp.concatenate(
-                [product[0:8] + product[8:16], product[16:]], axis=0)
-        return product
+        kind = lax.broadcasted_iota(jnp.int32, (PACK, 128), 1) & 3
+        return fewer_rows(jnp.where(kind >= 2, product, 0.0))
 
     def gather_a(call, values):
         for i, value in enumerate(values):
@@ -418,27 +442,12 @@
     def write_pixels(v, out):
         def step(b, carry):
             rows = pl.ds(pl.multiple_of(b * 128 + 8, 8), 128)
-            x = jnp.concatenate([vec[v, q, rows, :] for q in range(4)], axis=1)
+            x = jnp.concatenate([whole[v, q, rows, :] for q in range(4)], axis=1)
             high, low = halves(x)
             out[pl.ds(pl.multiple_of(b * 128, 128), 128), :] = dot(high, perm[1]) + dot(low, perm[1])
             return carry
 
         lax.fori_loop(0, 4, step, 0)
-
-    def patch_edges(v):
-        def step(i, carry):
-            for u in range(4):
-                tile = 1 + i * 4 + u
-                group, inner = place(tile)
-                rows = pl.ds(pl.multiple_of(tile * 8, 8), 8)
-                packed = vec[v, 4, pl.ds(pl.multiple_of(inner * 8, 8), 8), :]
-                packed = pltpu.roll(packed, 127 - 16 * group, axis=1)
-                for q in range(4):
-                    spun = packed if q == 0 else pltpu.roll(packed, 128 - 4 * q, axis=1)
-                    vec[v, q, rows, :] = jnp.where(edge, spun, vec[v, q, rows, :])
-            return carry
-
-        lax.fori_loop(0, 16, step, 0)
 
     unfold(0)
     mix()
@@ -446,21 +455,18 @@
     for copy in frame_moves:
         copy.wait()
     take_frames()
-    fold(0, -1.0, lambda rows, inside, old, out, sums: sums)
+    fold(0, -1.0, lambda rows, inside, old, out: (), 0)
     settle(1, exchange(1))
 
     unfold(1)
     mix()
 
-    def measure_w(rows, inside, old, out, sums):
-        rr, rw, _ = sums
-        for q in range(4):
-            rw = rw + old[q] * out[q]
-            if inside:
-                rr = rr + old[q] * old[q]
-        return rr, rw, zero8
-
-    rr, rw, _ = fold(1, 1.0, measure_w)
+    def measure_w(rows, inside, old, out):
+        rr = old[0] * old[0] + old[1] * old[1] + (old[2] * old[2] + old[3] * old[3])
+        rw = old[0] * out[0] + old[1] * out[1] + (old[2] * out[2] + old[3] * out[3])
+        return jnp.where(inside, rr, 0.0), rw
+
+    rr, rw = fold(1, 1.0, measure_w, 2)
     rw = rw + outer_columns(vec[1, 4, 0:PACK, :] * vec[2, 4, 0:PACK, :])
     moves = exchange(2)
     first_sums = gather_a(0, (rr, rw, zero8))
@@ -473,17 +479,15 @@
     rr, rw, _ = finish_sums(0, first_sums)
     alpha = rr / rw
 
-    def measure_z(rows, inside, old, out, sums):
-        ss, sw, sz = sums
+    def measure_z(rows, inside, old, out):
+        rate = jnp.broadcast_to(alpha[0:1], old[0].shape)
+        ss, sw, sz = 0.0, 0.0, 0.0
         for q in range(4):
-            s = vec[1, q, rows, :] - alpha * old[q]
-            sz = sz + s * out[q]
-            if inside:
-                ss = ss + s * s
-                sw = sw + s * old[q]
-        return ss, sw, sz
-
-    ss, sw, sz = fold(2, 1.0, measure_z)
+            s = whole[1, q, rows, :] - rate * old[q]
+            ss, sw, sz = ss + s * s, sw + s * old[q], sz + s * out[q]
+        return jnp.where(inside, ss, 0.0), jnp.where(inside, sw, 0.0), sz
+
+    ss, sw, sz = fold(2, 1.0, measure_z, 3)
     s_edge = vec[1, 4, 0:PACK, :] - alpha[0:1, :] * vec[2, 4, 0:PACK, :]
     sz = sz + outer_columns(s_edge * vec[3, 4, 0:PACK, :])
     last_sums = gather_a(1, (ss, sw, sz))
@@ -491,7 +495,7 @@
     write_pixels(2, w_out)
     last_sums = gather_b(1, last_sums)
     settle(3, moves)
-    patch_edges(3)
+    unfold(3, features=False)
     write_pixels(3, z_out)
     ss, sw, sz = finish_sums(1, last_sums)
     beta = ss / rr
@@ -513,6 +517,9 @@
         out_specs=(vmem, vmem, vmem, vmem),
         scratch_shapes=[
             pltpu.VMEM((4, 5, ROWS, 128), F32),
+            pltpu.VMEM((4, 4, ROWS, 128), F32),
+            pltpu.VMEM((ROWS, 128), F32),
+            pltpu.VMEM((8, ROWS, 128), F32),
             pltpu.VMEM((8, ROWS, 128), F32),
             pltpu.VMEM((8, ROWS, 128), F32),
             pltpu.VMEM((24 * FS, 128), F32),

time: 151 us -> 63.1 us (0.42)
  Pallas kernels: 143 us -> 54.3 us
    pallas_call x1, Pallas kernels: 143 us -> 54.3 us  [on_device(): pl.pallas_call(functools.partial(kernel, n_wide, n_narrow), out_shape=(im...]
where the time goes in v2:
time: 63.1 us; the launch traced here: 62.7 us
  Pallas kernels  54.3 us (86%)
  local copies, waits for them, and re-layouts  4.6 us (7%)
  other arithmetic  3.07 us (5%)
  between operations  0.67 us (1%)
    pallas_call x1, Pallas kernels, on_device(): pl.pallas_call(functools.partial(kernel, n_wide, n_narrow), out_shape=(im...  54.3 us
    unnamed x9, local copies, waits for them, and re-layouts  4.01 us
    add x1, other arithmetic, on_device(): return (guess + c1 * r - c2 * w, r - c1 * w + c2 * z)  3.07 us

profile of v2, /device:TPU:1, one launch (start us, length us, event | category | flops | bytes accessed | tf_op | source)
XLA Modules:
  0.0 62.7 jit_solution(5787648076978713652)
XLA Ops:
  0.6 0.0 copy-start.3
  0.6 0.8 %copy.7.shift = s32[1,256,2]{2,1,0:T(8,128)S(1)} copy(s32[1,256,2]{1,2,0:T(2,128)} %param.7) | data formatting | bytes 4096 | tf_op args[2]
  1.5 0.0 copy-done.3
  1.5 0.0 copy-start
  1.5 1.2 %copy-done = f32[512,512]{1,0:T(8,128)S(1)} copy-done((f32[512,512]{1,0:T(8,128)S(1)}, f32[512,512]{1,0:T(8,128)}, u32[]{:S(2)}) %copy-start) | copy-done | bytes 1048600
  2.7 0.0 copy-start.1
  2.7 1.0 %copy-done.1 = f32[1,8,128,128]{3,2,1,0:T(8,128)S(1)} copy-done((f32[1,8,128,128]{3,2,1,0:T(8,128)S(1)}, f32[1,8,128,128]{3,2,1,0:T(8,128)}, u32[]{:S(2)}) %copy-start.1) | copy-done | bytes 524312
  3.7 0.0 copy-start.2
  3.7 0.9 %copy-done.2 = f32[3,128,128]{2,1,0:T(8,128)S(1)} copy-done((f32[3,128,128]{2,1,0:T(8,128)S(1)}, f32[3,128,128]{2,1,0:T(8,128)}, u32[]{:S(2)}) %copy-start.2) | copy-done | bytes 196632
  4.7 54.3 %shard_map.68 = (f32[512,512]{1,0:T(8,128)S(1)}, f32[512,512]{1,0:T(8,128)S(1)}, f32[512,512]{1,0:T(8,128)S(1)}, f32[2,8,128]{2,1,0:T(8,128)S(1)}) custom-call(f32[1024,128]{1,0:T(8,128)S(1)} %bitcast.3, s32[1,256]{1,0:T(1,128)S(1)} %copy-done.3, s32[1,256,2]{2,1,0:T(8,128)S(1)} %copy.7.shift, f32[512,512]{1,0:T(8,128)S(1)} %copy-done, ...), custom_call_target="tpu_custom_call" | custom-call | tf_op jit(solution)/shard_map/pallas_call | solution.py:513
  59.0 0.6 fusion
  59.6 3.1 %multiply_add_fusion = (f32[512,512]{1,0:T(8,128)}, f32[512,512]{1,0:T(8,128)}) fusion(f32[512,512]{1,0:T(8,128)S(1)} %get-tuple-element.9, f32[512,512]{1,0:T(8,128)S(1)} %get-tuple-element.7, f32[512,512]{1,0:T(8,128)S(1)} %get-tuple-element.8, f32[]{:T(128)} %bitcast.2, f32[]{:T(128)} %bitcast.1, f32[512,512]{1,0:T(8,128)S(1)} %copy-done), kind=kLoop, calls=%fused_computation | loop fusion | flops 2097152 | bytes 6291464 | tf_op jit(solution)/shard_map/add | solution.py:541
Async XLA Ops:
  0.6 0.8 %copy-start.3 = (s32[1,256]{1,0:T(1,128)S(1)}, s32[1,256]{1,0:T(1,128)}, u32[]{:S(2)}) copy-start(s32[1,256]{1,0:T(1,128)} %anchor.1) | copy-start | bytes 3076
  1.5 1.2 %copy-start = (f32[512,512]{1,0:T(8,128)S(1)}, f32[512,512]{1,0:T(8,128)}, u32[]{:S(2)}) copy-start(f32[512,512]{1,0:T(8,128)} %guess.1) | copy-start | bytes 3145732
  2.7 1.0 %copy-start.1 = (f32[1,8,128,128]{3,2,1,0:T(8,128)S(1)}, f32[1,8,128,128]{3,2,1,0:T(8,128)}, u32[]{:S(2)}) copy-start(f32[1,8,128,128]{3,2,1,0:T(8,128)} %param.5) | copy-start | bytes 1572868
  3.7 0.9 %copy-start.2 = (f32[3,128,128]{2,1,0:T(8,128)S(1)}, f32[3,128,128]{2,1,0:T(8,128)}, u32[]{:S(2)}) copy-start(f32[3,128,128]{2,1,0:T(8,128)} %constant.2.clone.table) | copy-start | bytes 589828

commit v3 on v2

--- a/solution.py
+++ b/solution.py
@@ -51,8 +51,12 @@
     return jnp.dot(a, b, preferred_element_type=F32)
 
 
-def dot_nt(a, b, precision=None):
-    return lax.dot_general(a, b, (((1,), (1,)), ((), ())), precision=precision, preferred_element_type=F32)
+def exact_dot(a, b):
+    return jnp.dot(a, b, precision=HIGHEST, preferred_element_type=F32)
+
+
+def exact_dot_nt(a, b):
+    return lax.dot_general(a, b, (((1,), (1,)), ((), ())), precision=HIGHEST, preferred_element_type=F32)
 
 
 def total_of(x):
@@ -61,11 +65,11 @@
 
 def kernel(
     n_wide, n_narrow,
-    frames, anchor, shift, guess, table,
+    frames, anchor, shift, guess_hbm, table_hbm,
     r_out, w_out, z_out, coef,
-    vec, whole, wide_edges, feat, acc, more, frb, perm, lhs, lhsb,
+    guess, table, vec, whole, wide_edges, feat, acc, more, frb, perm, lhs, lhsb,
     from_side, from_row, from_corner, sums_a, sums_b,
-    send, recv, fsend, frecv, floc, asend, arecv, bsend, brecv,
+    send, recv, fsend, frecv, loc, asend, arecv, bsend, brecv,
 ):
     column = lax.axis_index("wide")
     row = lax.axis_index("narrow")
@@ -88,14 +92,20 @@
     for device in everyone:
         pl.semaphore_signal(barrier, inc=1, device_id=device, device_id_type=pl.DeviceIdType.MESH)
 
-    own = pltpu.make_async_copy(frames, frb.at[8 * FS : 16 * FS], floc)
-    own.start()
+    load_guess = pltpu.make_async_copy(guess_hbm, guess, loc.at[0])
+    load_table = pltpu.make_async_copy(table_hbm, table, loc.at[1])
+    own = pltpu.make_async_copy(frames, frb.at[8 * FS : 16 * FS], loc.at[2])
+    load_guess.start()
+    load_table.start()
 
     k_id = lax.broadcasted_iota(jnp.int32, (512, 128), 0)
     n_id = lax.broadcasted_iota(jnp.int32, (512, 128), 1)
-    for which, target in enumerate((128 * (k_id & 3) + (k_id >> 2), 4 * (k_id & 127) + (k_id >> 7))):
+
+    def permutation(which, target):
         for c in range(4):
             perm[which, :, c * 128 : c * 128 + 128] = jnp.where(n_id + 128 * c == target, 1.0, 0.0).astype(BF16)
+
+    permutation(0, 128 * (k_id & 3) + (k_id >> 2))
 
     zero8 = jnp.zeros((8, 128), F32)
 
@@ -128,18 +138,18 @@
     wide_edges[0:8, :] = zero8
     wide_edges[ROWS - 8 : ROWS, :] = zero8
 
-    def spread_guess(b, carry):
-        rows = pl.ds(pl.multiple_of(b * 128, 128), 128)
-        into = pl.ds(pl.multiple_of(b * 128 + 8, 8), 128)
-        high, low = halves(guess[rows, :])
+    def spread_guess(b):
+        into = slice(b * 128 + 8, b * 128 + 136)
+        high, low = halves(guess[b * 128 : b * 128 + 128, :])
         x = dot(high, perm[0]) + dot(low, perm[0])
         x = [x[:, q * 128 : q * 128 + 128] for q in range(4)]
         for q in range(4):
             vec[0, q, into, :] = x[q]
         wide_edges[into, :] = gather_edges([(4 * q + 1, x[q]) for q in range(4)])
-        return carry
-
-    lax.fori_loop(0, 4, spread_guess, 0)
+
+    load_guess.wait()
+    for b in range(4):
+        spread_guess(b)
     pack(0)
 
     pl.semaphore_wait(barrier, len(everyone))
@@ -209,6 +219,8 @@
             recv_sem=frecv.at[k], device_id=device, device_id_type=pl.DeviceIdType.MESH)
         copy.start()
         frame_moves.append(copy)
+    own.start()
+    permutation(1, 4 * (k_id & 127) + (k_id >> 7))
 
     n_frames = 8 * n_wide
     f_id = lax.broadcasted_iota(jnp.int32, (n_frames, 128), 0)
@@ -216,23 +228,28 @@
     slot = slot - (slot // 32) * 32
     wanted = lax.rem(slot + 8 * left, n_frames)
     pick = jnp.where((f_id == wanted) & (slot < 24), 1.0, 0.0).astype(BF16)
-    looks = jnp.where(jnp.broadcast_to(anchor[...], (16, n_frames)) == column, 1.0, 0.0).astype(BF16)
-    used = dot(looks, pick)[0:1]
-    codes = [shift[0, pl.ds(pl.multiple_of(8 * o, 8), 8), :] for o in (left, column, right)]
-    codes = jnp.concatenate((codes + [jnp.zeros((8, 2), jnp.int32)]) * 4, axis=0)
+    looks = jnp.where(jnp.broadcast_to(anchor[...], (16, n_frames)) == column, 1.0, 0.0)
+    code_row = lax.broadcasted_iota(jnp.int32, (16, n_frames), 0)
+    codes = jnp.where(code_row == 0, looks, jnp.where(
+        code_row == 1, jnp.broadcast_to(shift[0, 0:1, :], (16, n_frames)).astype(F32),
+        jnp.broadcast_to(shift[0, 1:2, :], (16, n_frames)).astype(F32)))
+    codes = dot(codes.astype(BF16), pick)
+    used = codes[0:1]
+    load_table.wait()
     lane128 = lax.broadcasted_iota(jnp.int32, (128, 128), 1)
-    one_a = jnp.where(codes[:, 0:1] == lane128, 1.0, 0.0)
-    one_b = jnp.where(codes[:, 1:2] == lane128, 1.0, 0.0)
+    sub128 = lax.broadcasted_iota(jnp.int32, (128, 128), 0)
+    one_a = jnp.where(jnp.broadcast_to(codes[1:2], (128, 128)).astype(jnp.int32) == sub128, 1.0, 0.0)
+    one_b = jnp.where(jnp.broadcast_to(codes[2:3], (128, 128)).astype(jnp.int32) == sub128, 1.0, 0.0)
     second = lax.rem(lane128 // 32, 2) == 1
-    tall = dot_nt(table[2], one_b, HIGHEST) * jnp.where(
-        second, dot_nt(table[1], one_a, HIGHEST), dot_nt(table[0], one_a, HIGHEST)) * used
+    tall = exact_dot(table[2], one_b) * jnp.where(
+        second, exact_dot(table[1], one_a), exact_dot(table[0], one_a)) * used
     for which, keep in enumerate((second, lane128 >= 0, jnp.logical_not(second))):
         kept = jnp.where(keep, tall, 0.0)
         high, low = halves(kept)
         lhsb[which, :, 0:128] = high
         lhsb[which, :, 128:256] = jnp.where(lane128 < 64, low.astype(F32), 0.0).astype(BF16)
         half = jnp.where(lane128 < 64, kept, 0.0)
-        high, low = halves(dot_nt(half, half, HIGHEST))
+        high, low = halves(exact_dot_nt(half, half))
         lhs[which, :, 0:128] = high
         lhs[which, :, 128:256] = high
         lhs[which, :, 256:384] = low
@@ -395,59 +412,50 @@
             total = total + x[k : k + 8]
         return total
 
+    def no_sums(rows, inside, old, out):
+        return ()
+
     def outer_columns(product):
         kind = lax.broadcasted_iota(jnp.int32, (PACK, 128), 1) & 3
         return fewer_rows(jnp.where(kind >= 2, product, 0.0))
 
-    def gather_a(call, values):
+    def gather(values, slots, mates, sent, landed):
         for i, value in enumerate(values):
-            sums_a[call, 0, i] = value
+            slots[0, i] = value
         copies = []
-        for k, device in enumerate(mates_a):
+        for k, device in enumerate(mates):
             copy = pltpu.make_async_remote_copy(
-                src_ref=sums_a.at[call, 0], dst_ref=sums_a.at[call, k + 1], send_sem=asend.at[call, k],
-                recv_sem=arecv.at[call, k], device_id=device, device_id_type=pl.DeviceIdType.MESH)
+                src_ref=slots.at[0], dst_ref=slots.at[k + 1], send_sem=sent.at[k],
+                recv_sem=landed.at[k], device_id=device, device_id_type=pl.DeviceIdType.MESH)
             copy.start()
             copies.append(copy)
         return copies
 
-    def gather_b(call, copies):
-        for copy in copies:
-            copy.wait()
-        for i in range(3):
-            value = sums_a[call, 0, i]
-            for k in range(len(mates_a)):
-                value = value + sums_a[call, k + 1, i]
-            sums_b[call, 0, i] = value
-        copies = []
-        for k, device in enumerate(mates_b):
-            copy = pltpu.make_async_remote_copy(
-                src_ref=sums_b.at[call, 0], dst_ref=sums_b.at[call, k + 1], send_sem=bsend.at[call, k],
-                recv_sem=brecv.at[call, k], device_id=device, device_id_type=pl.DeviceIdType.MESH)
-            copy.start()
-            copies.append(copy)
-        return copies
-
-    def finish_sums(call, copies):
+    def collect(copies, slots):
         for copy in copies:
             copy.wait()
         values = []
-        for i in range(3):
-            value = sums_b[call, 0, i]
-            for k in range(len(mates_b)):
-                value = value + sums_b[call, k + 1, i]
-            values.append(total_of(value))
+        for i in range(4):
+            value = slots[0, i]
+            for k in range(len(copies)):
+                value = value + slots[k + 1, i]
+            values.append(value)
         return values
 
+    def gather_a(values):
+        return gather(values, sums_a, mates_a, asend, arecv)
+
+    def gather_b(copies):
+        return gather(collect(copies, sums_a), sums_b, mates_b, bsend, brecv)
+
+    def finish_sums(copies):
+        return [total_of(value) for value in collect(copies, sums_b)]
+
     def write_pixels(v, out):
-        def step(b, carry):
-            rows = pl.ds(pl.multiple_of(b * 128 + 8, 8), 128)
-            x = jnp.concatenate([whole[v, q, rows, :] for q in range(4)], axis=1)
+        for b in range(4):
+            x = jnp.concatenate([whole[v, q, b * 128 + 8 : b * 128 + 136, :] for q in range(4)], axis=1)
             high, low = halves(x)
-            out[pl.ds(pl.multiple_of(b * 128, 128), 128), :] = dot(high, perm[1]) + dot(low, perm[1])
-            return carry
-
-        lax.fori_loop(0, 4, step, 0)
+            out[b * 128 : b * 128 + 128, :] = dot(high, perm[1]) + dot(low, perm[1])
 
     unfold(0)
     mix()
@@ -455,7 +463,7 @@
     for copy in frame_moves:
         copy.wait()
     take_frames()
-    fold(0, -1.0, lambda rows, inside, old, out: (), 0)
+    fold(0, -1.0, no_sums, 0)
     settle(1, exchange(1))
 
     unfold(1)
@@ -469,53 +477,70 @@
     rr, rw = fold(1, 1.0, measure_w, 2)
     rw = rw + outer_columns(vec[1, 4, 0:PACK, :] * vec[2, 4, 0:PACK, :])
     moves = exchange(2)
-    first_sums = gather_a(0, (rr, rw, zero8))
     write_pixels(1, r_out)
     settle(2, moves)
-    first_sums = gather_b(0, first_sums)
 
     unfold(2)
     mix()
-    rr, rw, _ = finish_sums(0, first_sums)
-    alpha = rr / rw
-
-    def measure_z(rows, inside, old, out):
-        rate = jnp.broadcast_to(alpha[0:1], old[0].shape)
-        ss, sw, sz = 0.0, 0.0, 0.0
-        for q in range(4):
-            s = whole[1, q, rows, :] - rate * old[q]
-            ss, sw, sz = ss + s * s, sw + s * old[q], sz + s * out[q]
-        return jnp.where(inside, ss, 0.0), jnp.where(inside, sw, 0.0), sz
-
-    ss, sw, sz = fold(2, 1.0, measure_z, 3)
-    s_edge = vec[1, 4, 0:PACK, :] - alpha[0:1, :] * vec[2, 4, 0:PACK, :]
-    sz = sz + outer_columns(s_edge * vec[3, 4, 0:PACK, :])
-    last_sums = gather_a(1, (ss, sw, sz))
+    ww = jnp.zeros((8, 128), F32)
+    for q in range(4):
+        own_rows = whole[2, q, 8 : ROWS - 8, :]
+        ww = ww + fewer_rows(own_rows * own_rows)
+    wz = DAMP * ww
+    for f in range(8):
+        wz = wz + fewer_rows(feat[f] * acc[f])
+    sums = gather_a((rr, rw, ww, wz))
+    fold(2, 1.0, no_sums, 0)
     moves = exchange(3)
+    sums = gather_b(sums)
     write_pixels(2, w_out)
-    last_sums = gather_b(1, last_sums)
     settle(3, moves)
     unfold(3, features=False)
     write_pixels(3, z_out)
-    ss, sw, sz = finish_sums(1, last_sums)
+    rr, rw, ww, wz = finish_sums(sums)
+    alpha = rr / rw
+    ss = alpha * alpha * ww - rr
+    sw = rw - alpha * ww
     beta = ss / rr
-    curve = (sw - alpha * sz) + 2.0 * beta * sw + beta * beta * rw
+    curve = (sw - alpha * (ww - alpha * wz)) + 2.0 * beta * sw + beta * beta * rw
     step = ss / curve
     coef[0] = alpha + step * (1.0 + beta)
     coef[1] = step * alpha
 
 
+def closing(guess_hbm, r, w, z, coef, solution_hbm, residual_hbm, guess, first, second, sems):
+    load = pltpu.make_async_copy(guess_hbm, guess, sems.at[0])
+    load.start()
+    c1, c2 = coef[0, 0:1, 0:1], coef[1, 0:1, 0:1]
+    stores = []
+    for b in range(4):
+        rows = slice(b * 128, b * 128 + 128)
+        second[rows, :] = r[rows, :] - c1 * w[rows, :] + c2 * z[rows, :]
+        stores.append(pltpu.make_async_copy(second.at[rows], residual_hbm.at[rows], sems.at[1 + b]))
+        stores[-1].start()
+    load.wait()
+    for b in range(4):
+        rows = slice(b * 128, b * 128 + 128)
+        first[rows, :] = guess[rows, :] + c1 * r[rows, :] - c2 * w[rows, :]
+        stores.append(pltpu.make_async_copy(first.at[rows], solution_hbm.at[rows], sems.at[5 + b]))
+        stores[-1].start()
+    for store in stores:
+        store.wait()
+
+
 def on_device(n_wide, n_narrow, frames, anchor, shift, guess):
-    vmem = pl.BlockSpec(memory_space=pltpu.VMEM)
+    vmem, hbm = pl.BlockSpec(memory_space=pltpu.VMEM), pl.BlockSpec(memory_space=pltpu.HBM)
     image = jax.ShapeDtypeStruct((TS, TS), F32)
     dma = pltpu.SemaphoreType.DMA
     n_a, n_b = 2 * n_narrow, n_wide // 2
     r, w, z, coef = pl.pallas_call(
         functools.partial(kernel, n_wide, n_narrow),
         out_shape=(image, image, image, jax.ShapeDtypeStruct((2, 8, 128), F32)),
-        in_specs=[pl.BlockSpec(memory_space=pl.ANY), vmem, vmem, vmem, vmem],
+        in_specs=[hbm, vmem, vmem, hbm, hbm],
         out_specs=(vmem, vmem, vmem, vmem),
         scratch_shapes=[
+            pltpu.VMEM((TS, TS), F32),
+            pltpu.VMEM((3, 128, 128), F32),
             pltpu.VMEM((4, 5, ROWS, 128), F32),
             pltpu.VMEM((4, 4, ROWS, 128), F32),
             pltpu.VMEM((ROWS, 128), F32),
@@ -529,16 +554,21 @@
             pltpu.VMEM((4, 2, PACK, 128), F32),
             pltpu.VMEM((4, 2, 5, 16, 128), F32),
             pltpu.VMEM((4, 4, 16, 128), F32),
-            pltpu.VMEM((2, n_a, 3, 8, 128), F32),
-            pltpu.VMEM((2, n_b, 3, 8, 128), F32),
-            dma((4, 8)), dma((4, 8)), dma((2,)), dma((2,)), dma,
-            dma((2, n_a)), dma((2, n_a)), dma((2, n_b)), dma((2, n_b)),
+            pltpu.VMEM((n_a, 4, 8, 128), F32),
+            pltpu.VMEM((n_b, 4, 8, 128), F32),
+            dma((4, 8)), dma((4, 8)), dma((2,)), dma((2,)), dma((3,)),
+            dma((n_a,)), dma((n_a,)), dma((n_b,)), dma((n_b,)),
         ],
         compiler_params=pltpu.CompilerParams(
             collective_id=0, has_side_effects=True, vmem_limit_bytes=48 * 2**20),
-    )(frames.reshape(8 * FS, FS), anchor, shift, guess, jnp.asarray(tables()))
-    c1, c2 = coef[0, 0, 0], coef[1, 0, 0]
-    return guess + c1 * r - c2 * w, r - c1 * w + c2 * z
+    )(frames.reshape(8 * FS, FS), anchor, shift.transpose(0, 2, 1), guess, jnp.asarray(tables()))
+    return pl.pallas_call(
+        closing,
+        out_shape=(image, image),
+        in_specs=[hbm, vmem, vmem, vmem, vmem],
+        out_specs=(hbm, hbm),
+        scratch_shapes=[pltpu.VMEM((TS, TS), F32)] * 3 + [dma((9,))],
+    )(guess, r, w, z, coef)
 
 
 def solution(mesh):

time: 63.1 us -> 62.8 us (level)
  other arithmetic: 3.07 us -> 0 us
  local copies, waits for them, and re-layouts: 4.6 us -> 7.42 us
    pallas_call x1, Pallas kernels: 54.3 us -> 49.7 us  [on_device(): pl.pallas_call(functools.partial(kernel, n_wide, n_narrow), out_shape=(im...]
    pallas_call x0 -> x1, Pallas kernels: none -> 4.53 us  [on_device(): pl.pallas_call(closing, out_shape=(image, image), in_specs=[hbm, vmem, vm...]
    unnamed x9 -> x18, local copies, waits for them, and re-layouts: 4.01 us -> 7.42 us
    add x1 -> x0, other arithmetic: 3.07 us -> none  [on_device(): return (guess + c1 * r - c2 * w, r - c1 * w + c2 * z)]
where the time goes in v3:
time: 62.8 us; the launch traced here: 62.5 us
  Pallas kernels  54.2 us (86%)
  local copies, waits for them, and re-layouts  7.42 us (12%)
  between operations  0.83 us (1%)
    pallas_call x1, Pallas kernels, on_device(): pl.pallas_call(functools.partial(kernel, n_wide, n_narrow), out_shape=(im...  49.7 us
    unnamed x18, local copies, waits for them, and re-layouts  7.42 us
    pallas_call x1, Pallas kernels, on_device(): pl.pallas_call(closing, out_shape=(image, image), in_specs=[hbm, vmem, vm...  4.53 us

profile of v3, /device:TPU:1, one launch (start us, length us, event | category | flops | bytes accessed | tf_op | source)
XLA Modules:
  0.0 62.5 jit_solution(14648680773429567596)
XLA Ops:
  0.6 0.0 copy-start.7
  0.6 0.0 copy-start.8
  0.6 0.7 %copy-done.7 = s32[1,256,2]{1,2,0:T(2,128)S(1)} copy-done((s32[1,256,2]{1,2,0:T(2,128)S(1)}, s32[1,256,2]{1,2,0:T(2,128)}, u32[]{:S(2)}) %copy-start.7) | copy-done | bytes 2072
  1.3 0.0 copy-done.8
  1.3 0.0 copy-start
  1.3 1.2 %copy-done = f32[512,512]{1,0:T(8,128)S(1)} copy-done((f32[512,512]{1,0:T(8,128)S(1)}, f32[512,512]{1,0:T(8,128)}, u32[]{:S(2)}) %copy-start) | copy-done | bytes 1048600
  2.6 0.0 copy-start.4
  2.6 1.0 %copy-done.4 = f32[1,8,128,128]{3,2,1,0:T(8,128)S(1)} copy-done((f32[1,8,128,128]{3,2,1,0:T(8,128)S(1)}, f32[1,8,128,128]{3,2,1,0:T(8,128)}, u32[]{:S(2)}) %copy-start.4) | copy-done | bytes 524312
  3.6 0.0 copy-start.5
  3.6 0.9 %copy-done.5 = f32[3,128,128]{2,1,0:T(8,128)S(1)} copy-done((f32[3,128,128]{2,1,0:T(8,128)S(1)}, f32[3,128,128]{2,1,0:T(8,128)}, u32[]{:S(2)}) %copy-start.5) | copy-done | bytes 196632
  4.5 49.7 %shard_map.68 = (f32[512,512]{1,0:T(8,128)S(1)}, f32[512,512]{1,0:T(8,128)S(1)}, f32[512,512]{1,0:T(8,128)S(1)}, f32[2,8,128]{2,1,0:T(8,128)S(1)}) custom-call(f32[1024,128]{1,0:T(8,128)S(1)} %bitcast.2, s32[1,256]{1,0:T(1,128)S(1)} %copy-done.8, s32[1,2,256]{2,1,0:T(2,128)S(1)} %bitcast.3, f32[512,512]{1,0:T(8,128)S(1)} %copy-done, f32[3,128,128]{2,1,0:T(8,128)S(1)} %copy-done.5), custom_call_target="tpu_custom_call" | custom-call | tf_op jit(solution)/shard_map/pallas_call | solution.py:536
  54.2 0.0 copy-start.1
  54.2 1.0 %copy-done.1 = f32[512,512]{1,0:T(8,128)} copy-done((f32[512,512]{1,0:T(8,128)}, f32[512,512]{1,0:T(8,128)S(1)}, u32[]{:S(2)}) %copy-start.1) | copy-done | bytes 1048600
  55.2 0.0 copy-start.2
  55.2 1.0 %copy-done.2 = f32[512,512]{1,0:T(8,128)} copy-done((f32[512,512]{1,0:T(8,128)}, f32[512,512]{1,0:T(8,128)S(1)}, u32[]{:S(2)}) %copy-start.2) | copy-done | bytes 1048600
  56.2 0.0 copy-start.3
  56.2 1.0 %copy-done.3 = f32[512,512]{1,0:T(8,128)} copy-done((f32[512,512]{1,0:T(8,128)}, f32[512,512]{1,0:T(8,128)S(1)}, u32[]{:S(2)}) %copy-start.3) | copy-done | bytes 1048600
  57.2 0.0 copy-start.6
  57.2 0.6 copy-done.6
  57.8 4.5 %shard_map.69 = (f32[512,512]{1,0:T(8,128)}, f32[512,512]{1,0:T(8,128)}) custom-call(f32[512,512]{1,0:T(8,128)} %guess_hbm.3, f32[512,512]{1,0:T(8,128)} %copy-done.1, f32[512,512]{1,0:T(8,128)} %copy-done.2, f32[512,512]{1,0:T(8,128)} %copy-done.3, f32[2,8,128]{2,1,0:T(8,128)} %copy-done.6), custom_call_target="tpu_custom_call" | custom-call | tf_op jit(solution)/shard_map/pallas_call | solution.py:565
Async XLA Ops:
  0.6 0.7 %copy-start.7 = (s32[1,256,2]{1,2,0:T(2,128)S(1)}, s32[1,256,2]{1,2,0:T(2,128)}, u32[]{:S(2)}) copy-start(s32[1,256,2]{1,2,0:T(2,128)} %param.7) | copy-start | bytes 6148
  0.6 0.7 %copy-start.8 = (s32[1,256]{1,0:T(1,128)S(1)}, s32[1,256]{1,0:T(1,128)}, u32[]{:S(2)}) copy-start(s32[1,256]{1,0:T(1,128)} %anchor.1) | copy-start | bytes 3076
  1.3 1.2 %copy-start = (f32[512,512]{1,0:T(8,128)S(1)}, f32[512,512]{1,0:T(8,128)}, u32[]{:S(2)}) copy-start(f32[512,512]{1,0:T(8,128)} %guess_hbm.3) | copy-start | bytes 3145732
  2.6 1.0 %copy-start.4 = (f32[1,8,128,128]{3,2,1,0:T(8,128)S(1)}, f32[1,8,128,128]{3,2,1,0:T(8,128)}, u32[]{:S(2)}) copy-start(f32[1,8,128,128]{3,2,1,0:T(8,128)} %param.5) | copy-start | bytes 1572868
  3.6 0.9 %copy-start.5 = (f32[3,128,128]{2,1,0:T(8,128)S(1)}, f32[3,128,128]{2,1,0:T(8,128)}, u32[]{:S(2)}) copy-start(f32[3,128,128]{2,1,0:T(8,128)} %constant.2.clone.table_hbm) | copy-start | bytes 589828
  54.2 1.0 %copy-start.1 = (f32[512,512]{1,0:T(8,128)}, f32[512,512]{1,0:T(8,128)S(1)}, u32[]{:S(2)}) copy-start(f32[512,512]{1,0:T(8,128)S(1)} %get-tuple-element.6.r) | copy-start | bytes 3145732
  55.2 1.0 %copy-start.2 = (f32[512,512]{1,0:T(8,128)}, f32[512,512]{1,0:T(8,128)S(1)}, u32[]{:S(2)}) copy-start(f32[512,512]{1,0:T(8,128)S(1)} %get-tuple-element.7.w) | copy-start | bytes 3145732
  56.2 1.0 %copy-start.3 = (f32[512,512]{1,0:T(8,128)}, f32[512,512]{1,0:T(8,128)S(1)}, u32[]{:S(2)}) copy-start(f32[512,512]{1,0:T(8,128)S(1)} %get-tuple-element.8.z) | copy-start | bytes 3145732
  57.2 0.6 copy-start.6

commit v4 on v3

--- a/solution.py
+++ b/solution.py
@@ -21,6 +21,8 @@
 UNFOLD = 264
 FOLD = 264
 MIX = 32
+CLOSE = 4
+VMEM_BYTES = 62 * 2**20
 HIGHEST = lax.Precision.HIGHEST
 
 
@@ -66,10 +68,10 @@
 def kernel(
     n_wide, n_narrow,
     frames, anchor, shift, guess_hbm, table_hbm,
-    r_out, w_out, z_out, coef,
-    guess, table, vec, whole, wide_edges, feat, acc, more, frb, perm, lhs, lhsb,
+    r_hbm, w_hbm, z_hbm, coef,
+    guess, pixels, table, vec, whole, wide_edges, feat, acc, more, frb, perm, lhs, lhsb,
     from_side, from_row, from_corner, sums_a, sums_b,
-    send, recv, fsend, frecv, loc, asend, arecv, bsend, brecv,
+    send, recv, fsend, frecv, loc, stores, asend, arecv, bsend, brecv,
 ):
     column = lax.axis_index("wide")
     row = lax.axis_index("narrow")
@@ -453,9 +455,13 @@
 
     def write_pixels(v, out):
         for b in range(4):
+            rows = slice(b * 128, b * 128 + 128)
             x = jnp.concatenate([whole[v, q, b * 128 + 8 : b * 128 + 136, :] for q in range(4)], axis=1)
             high, low = halves(x)
-            out[b * 128 : b * 128 + 128, :] = dot(high, perm[1]) + dot(low, perm[1])
+            pixels[v - 1, rows, :] = dot(high, perm[1]) + dot(low, perm[1])
+        store = pltpu.make_async_copy(pixels.at[v - 1], out, stores.at[v - 1])
+        store.start()
+        return store
 
     unfold(0)
     mix()
@@ -477,7 +483,7 @@
     rr, rw = fold(1, 1.0, measure_w, 2)
     rw = rw + outer_columns(vec[1, 4, 0:PACK, :] * vec[2, 4, 0:PACK, :])
     moves = exchange(2)
-    write_pixels(1, r_out)
+    written = [write_pixels(1, r_hbm)]
     settle(2, moves)
 
     unfold(2)
@@ -493,10 +499,10 @@
     fold(2, 1.0, no_sums, 0)
     moves = exchange(3)
     sums = gather_b(sums)
-    write_pixels(2, w_out)
+    written.append(write_pixels(2, w_hbm))
     settle(3, moves)
     unfold(3, features=False)
-    write_pixels(3, z_out)
+    written.append(write_pixels(3, z_hbm))
     rr, rw, ww, wz = finish_sums(sums)
     alpha = rr / rw
     ss = alpha * alpha * ww - rr
@@ -506,26 +512,32 @@
     step = ss / curve
     coef[0] = alpha + step * (1.0 + beta)
     coef[1] = step * alpha
-
-
-def closing(guess_hbm, r, w, z, coef, solution_hbm, residual_hbm, guess, first, second, sems):
-    load = pltpu.make_async_copy(guess_hbm, guess, sems.at[0])
-    load.start()
+    for store in written:
+        store.wait()
+
+
+def closing(guess_hbm, r_hbm, w_hbm, z_hbm, coef, solution_hbm, residual_hbm, held, made, loads, stores):
+    sources = (r_hbm, w_hbm, z_hbm, guess_hbm)
+    copies = {}
+    for b in range(CLOSE):
+        rows = slice(b * (TS // CLOSE), (b + 1) * (TS // CLOSE))
+        for k, source in enumerate(sources):
+            copies[b, k] = pltpu.make_async_copy(source.at[rows], held.at[k, rows], loads.at[b, k])
+            copies[b, k].start()
     c1, c2 = coef[0, 0:1, 0:1], coef[1, 0:1, 0:1]
-    stores = []
-    for b in range(4):
-        rows = slice(b * 128, b * 128 + 128)
-        second[rows, :] = r[rows, :] - c1 * w[rows, :] + c2 * z[rows, :]
-        stores.append(pltpu.make_async_copy(second.at[rows], residual_hbm.at[rows], sems.at[1 + b]))
-        stores[-1].start()
-    load.wait()
-    for b in range(4):
-        rows = slice(b * 128, b * 128 + 128)
-        first[rows, :] = guess[rows, :] + c1 * r[rows, :] - c2 * w[rows, :]
-        stores.append(pltpu.make_async_copy(first.at[rows], solution_hbm.at[rows], sems.at[5 + b]))
-        stores[-1].start()
-    for store in stores:
-        store.wait()
+    writes = []
+    for b in range(CLOSE):
+        rows = slice(b * (TS // CLOSE), (b + 1) * (TS // CLOSE))
+        for k in range(4):
+            copies[b, k].wait()
+        r, w = held[0, rows, :], held[1, rows, :]
+        made[1, rows, :] = r - c1 * w + c2 * held[2, rows, :]
+        made[0, rows, :] = held[3, rows, :] + c1 * r - c2 * w
+        for k, target in enumerate((solution_hbm, residual_hbm)):
+            writes.append(pltpu.make_async_copy(made.at[k, rows], target.at[rows], stores.at[b, k]))
+            writes[-1].start()
+    for write in writes:
+        write.wait()
 
 
 def on_device(n_wide, n_narrow, frames, anchor, shift, guess):
@@ -537,9 +549,10 @@
         functools.partial(kernel, n_wide, n_narrow),
         out_shape=(image, image, image, jax.ShapeDtypeStruct((2, 8, 128), F32)),
         in_specs=[hbm, vmem, vmem, hbm, hbm],
-        out_specs=(vmem, vmem, vmem, vmem),
+        out_specs=(hbm, hbm, hbm, vmem),
         scratch_shapes=[
             pltpu.VMEM((TS, TS), F32),
+            pltpu.VMEM((3, TS, TS), F32),
             pltpu.VMEM((3, 128, 128), F32),
             pltpu.VMEM((4, 5, ROWS, 128), F32),
             pltpu.VMEM((4, 4, ROWS, 128), F32),
@@ -556,18 +569,19 @@
             pltpu.VMEM((4, 4, 16, 128), F32),
             pltpu.VMEM((n_a, 4, 8, 128), F32),
             pltpu.VMEM((n_b, 4, 8, 128), F32),
-            dma((4, 8)), dma((4, 8)), dma((2,)), dma((2,)), dma((3,)),
+            dma((4, 8)), dma((4, 8)), dma((2,)), dma((2,)), dma((3,)), dma((3,)),
             dma((n_a,)), dma((n_a,)), dma((n_b,)), dma((n_b,)),
         ],
         compiler_params=pltpu.CompilerParams(
-            collective_id=0, has_side_effects=True, vmem_limit_bytes=48 * 2**20),
+            collective_id=0, has_side_effects=True, vmem_limit_bytes=VMEM_BYTES),
     )(frames.reshape(8 * FS, FS), anchor, shift.transpose(0, 2, 1), guess, jnp.asarray(tables()))
     return pl.pallas_call(
         closing,
         out_shape=(image, image),
-        in_specs=[hbm, vmem, vmem, vmem, vmem],
+        in_specs=[hbm, hbm, hbm, hbm, vmem],
         out_specs=(hbm, hbm),
-        scratch_shapes=[pltpu.VMEM((TS, TS), F32)] * 3 + [dma((9,))],
+        scratch_shapes=[pltpu.VMEM((4, TS, TS), F32), pltpu.VMEM((2, TS, TS), F32), dma((CLOSE, 4)), dma((CLOSE, 2))],
+        compiler_params=pltpu.CompilerParams(vmem_limit_bytes=VMEM_BYTES),
     )(guess, r, w, z, coef)
 
 

time: 62.8 us -> 56.1 us (0.89)
  local copies, waits for them, and re-layouts: 7.42 us -> 0 us
  Pallas kernels: 54.2 us -> 55.1 us
    unnamed x18 -> x0, local copies, waits for them, and re-layouts: 7.42 us -> none
    pallas_call x1, Pallas kernels: 49.7 us -> 51.2 us  [on_device(): pl.pallas_call(functools.partial(kernel, n_wide, n_narrow), out_shape=(im...]
    pallas_call x1, Pallas kernels: 4.53 us -> 3.9 us  [on_device(): pl.pallas_call(closing, out_shape=(image, image), in_specs=[hbm, hbm, hbm...]
where the time goes in v4:
time: 56.1 us; the launch traced here: 55.9 us
  Pallas kernels  55.1 us (98%)
  between operations  0.8 us (1%)
    pallas_call x1, Pallas kernels, on_device(): pl.pallas_call(functools.partial(kernel, n_wide, n_narrow), out_shape=(im...  51.2 us
    pallas_call x1, Pallas kernels, on_device(): pl.pallas_call(closing, out_shape=(image, image), in_specs=[hbm, hbm, hbm...  3.9 us

profile of v4, /device:TPU:1, one launch (start us, length us, event | category | flops | bytes accessed | tf_op | source)
XLA Modules:
  0.0 55.9 jit_solution(18052262285529552942)
XLA Ops:
  0.6 51.2 %shard_map.68 = (f32[512,512]{1,0:T(8,128)}, f32[512,512]{1,0:T(8,128)}, f32[512,512]{1,0:T(8,128)}, f32[2,8,128]{2,1,0:T(8,128)}) custom-call(f32[1024,128]{1,0:T(8,128)} %bitcast.2, s32[1,256]{1,0:T(1,128)} %anchor.1, s32[1,2,256]{2,1,0:T(2,128)} %bitcast.3, f32[512,512]{1,0:T(8,128)} %guess_hbm.3, f32[3,128,128]{2,1,0:T(8,128)} %constant.2.clone.table_hbm), custom_call_target="tpu_custom_call" | custom-call | tf_op jit(solution)/shard_map/pallas_call | solution.py:548
  51.8 3.9 %shard_map.69 = (f32[512,512]{1,0:T(8,128)}, f32[512,512]{1,0:T(8,128)}) custom-call(f32[512,512]{1,0:T(8,128)} %guess_hbm.3, f32[512,512]{1,0:T(8,128)} %get-tuple-element.6.r_hbm, f32[512,512]{1,0:T(8,128)} %get-tuple-element.7.w_hbm, f32[512,512]{1,0:T(8,128)} %get-tuple-element.8.z_hbm, f32[2,8,128]{2,1,0:T(8,128)} %get-tuple-element.9.coef), custom_call_target="tpu_custom_call" | custom-call | tf_op jit(solution)/shard_map/pallas_call | solution.py:578

commit v5 on v4

--- a/solution.py
+++ b/solution.py
@@ -18,9 +18,9 @@
 PACK = GROUP * 8
 F32 = jnp.float32
 BF16 = jnp.bfloat16
-UNFOLD = 264
-FOLD = 264
-MIX = 32
+UNFOLD = 528
+FOLD = 528
+MIX = 64
 CLOSE = 4
 VMEM_BYTES = 62 * 2**20
 HIGHEST = lax.Precision.HIGHEST
@@ -59,10 +59,6 @@
 
 def exact_dot_nt(a, b):
     return lax.dot_general(a, b, (((1,), (1,)), ((), ())), precision=HIGHEST, preferred_element_type=F32)
-
-
-def total_of(x):
-    return jnp.broadcast_to(jnp.sum(x, axis=(0, 1), keepdims=True), (8, 128))
 
 
 def kernel(
@@ -421,9 +417,8 @@
         kind = lax.broadcasted_iota(jnp.int32, (PACK, 128), 1) & 3
         return fewer_rows(jnp.where(kind >= 2, product, 0.0))
 
-    def gather(values, slots, mates, sent, landed):
-        for i, value in enumerate(values):
-            slots[0, i] = value
+    def gather(value, slots, mates, sent, landed):
+        slots[0] = value
         copies = []
         for k, device in enumerate(mates):
             copy = pltpu.make_async_remote_copy(
@@ -436,22 +431,21 @@
     def collect(copies, slots):
         for copy in copies:
             copy.wait()
-        values = []
-        for i in range(4):
-            value = slots[0, i]
-            for k in range(len(copies)):
-                value = value + slots[k + 1, i]
-            values.append(value)
-        return values
+        value = slots[0]
+        for k in range(len(copies)):
+            value = value + slots[k + 1]
+        return value
 
     def gather_a(values):
-        return gather(values, sums_a, mates_a, asend, arecv)
+        lines = [jnp.sum(value, axis=0, keepdims=True) for value in values]
+        return gather(jnp.concatenate(lines + [zero8[0:4]], axis=0), sums_a, mates_a, asend, arecv)
 
     def gather_b(copies):
         return gather(collect(copies, sums_a), sums_b, mates_b, bsend, brecv)
 
     def finish_sums(copies):
-        return [total_of(value) for value in collect(copies, sums_b)]
+        totals = jnp.broadcast_to(jnp.sum(collect(copies, sums_b), axis=1, keepdims=True), (8, 128))
+        return [jnp.broadcast_to(totals[i : i + 1], (8, 128)) for i in range(4)]
 
     def write_pixels(v, out):
         for b in range(4):
@@ -567,8 +561,8 @@
             pltpu.VMEM((4, 2, PACK, 128), F32),
             pltpu.VMEM((4, 2, 5, 16, 128), F32),
             pltpu.VMEM((4, 4, 16, 128), F32),
-            pltpu.VMEM((n_a, 4, 8, 128), F32),
-            pltpu.VMEM((n_b, 4, 8, 128), F32),
+            pltpu.VMEM((n_a, 8, 128), F32),
+            pltpu.VMEM((n_b, 8, 128), F32),
             dma((4, 8)), dma((4, 8)), dma((2,)), dma((2,)), dma((3,)), dma((3,)),
             dma((n_a,)), dma((n_a,)), dma((n_b,)), dma((n_b,)),
         ],

time: 56.1 us -> 52.9 us (0.943)
  Pallas kernels: 55.1 us -> 51.4 us
    pallas_call x1, Pallas kernels: 51.2 us -> 47.5 us  [on_device(): pl.pallas_call(functools.partial(kernel, n_wide, n_narrow), out_shape=(im...]
where the time goes in v5:
time: 52.9 us; the launch traced here: 52.2 us
  Pallas kernels  51.4 us (97%)
  between operations  0.8 us (2%)
    pallas_call x1, Pallas kernels, on_device(): pl.pallas_call(functools.partial(kernel, n_wide, n_narrow), out_shape=(im...  47.5 us
    pallas_call x1, Pallas kernels, on_device(): pl.pallas_call(closing, out_shape=(image, image), in_specs=[hbm, hbm, hbm...  3.9 us

profile of v5, /device:TPU:1, one launch (start us, length us, event | category | flops | bytes accessed | tf_op | source)
XLA Modules:
  0.0 52.2 jit_solution(15041547299100193436)
XLA Ops:
  0.6 47.5 %shard_map.68 = (f32[512,512]{1,0:T(8,128)}, f32[512,512]{1,0:T(8,128)}, f32[512,512]{1,0:T(8,128)}, f32[2,8,128]{2,1,0:T(8,128)}) custom-call(f32[1024,128]{1,0:T(8,128)} %bitcast.2, s32[1,256]{1,0:T(1,128)} %anchor.1, s32[1,2,256]{2,1,0:T(2,128)} %bitcast.3, f32[512,512]{1,0:T(8,128)} %guess_hbm.3, f32[3,128,128]{2,1,0:T(8,128)} %constant.2.clone.table_hbm), custom_call_target="tpu_custom_call" | custom-call | tf_op jit(solution)/shard_map/pallas_call | solution.py:542
  48.1 3.9 %shard_map.69 = (f32[512,512]{1,0:T(8,128)}, f32[512,512]{1,0:T(8,128)}) custom-call(f32[512,512]{1,0:T(8,128)} %guess_hbm.3, f32[512,512]{1,0:T(8,128)} %get-tuple-element.6.r_hbm, f32[512,512]{1,0:T(8,128)} %get-tuple-element.7.w_hbm, f32[512,512]{1,0:T(8,128)} %get-tuple-element.8.z_hbm, f32[2,8,128]{2,1,0:T(8,128)} %get-tuple-element.9.coef), custom_call_target="tpu_custom_call" | custom-call | tf_op jit(solution)/shard_map/pallas_call | solution.py:572

commit v6 on v5

--- a/solution.py
+++ b/solution.py
@@ -22,6 +22,7 @@
 FOLD = 528
 MIX = 64
 CLOSE = 4
+PARTS = 4
 VMEM_BYTES = 62 * 2**20
 HIGHEST = lax.Precision.HIGHEST
 
@@ -64,7 +65,7 @@
 def kernel(
     n_wide, n_narrow,
     frames, anchor, shift, guess_hbm, table_hbm,
-    r_hbm, w_hbm, z_hbm, coef,
+    solution_hbm, residual_hbm,
     guess, pixels, table, vec, whole, wide_edges, feat, acc, more, frb, perm, lhs, lhsb,
     from_side, from_row, from_corner, sums_a, sums_b,
     send, recv, fsend, frecv, loc, stores, asend, arecv, bsend, brecv,
@@ -165,7 +166,8 @@
             (edges.at[0:16], from_corner.at[v, 3]),
         ]
         copies = []
-        for k, (source, target) in enumerate(parts):
+        for k in (4, 5, 6, 7, 0, 1, 2, 3):
+            source, target = parts[k]
             copy = pltpu.make_async_remote_copy(
                 src_ref=source, dst_ref=target, send_sem=send.at[v, k], recv_sem=recv.at[v, k],
                 device_id=near[k], device_id_type=pl.DeviceIdType.MESH)
@@ -447,15 +449,12 @@
         totals = jnp.broadcast_to(jnp.sum(collect(copies, sums_b), axis=1, keepdims=True), (8, 128))
         return [jnp.broadcast_to(totals[i : i + 1], (8, 128)) for i in range(4)]
 
-    def write_pixels(v, out):
+    def write_pixels(v):
         for b in range(4):
             rows = slice(b * 128, b * 128 + 128)
             x = jnp.concatenate([whole[v, q, b * 128 + 8 : b * 128 + 136, :] for q in range(4)], axis=1)
             high, low = halves(x)
             pixels[v - 1, rows, :] = dot(high, perm[1]) + dot(low, perm[1])
-        store = pltpu.make_async_copy(pixels.at[v - 1], out, stores.at[v - 1])
-        store.start()
-        return store
 
     unfold(0)
     mix()
@@ -477,7 +476,7 @@
     rr, rw = fold(1, 1.0, measure_w, 2)
     rw = rw + outer_columns(vec[1, 4, 0:PACK, :] * vec[2, 4, 0:PACK, :])
     moves = exchange(2)
-    written = [write_pixels(1, r_hbm)]
+    write_pixels(1)
     settle(2, moves)
 
     unfold(2)
@@ -492,11 +491,11 @@
     sums = gather_a((rr, rw, ww, wz))
     fold(2, 1.0, no_sums, 0)
     moves = exchange(3)
+    write_pixels(2)
     sums = gather_b(sums)
-    written.append(write_pixels(2, w_hbm))
     settle(3, moves)
     unfold(3, features=False)
-    written.append(write_pixels(3, z_hbm))
+    write_pixels(3)
     rr, rw, ww, wz = finish_sums(sums)
     alpha = rr / rw
     ss = alpha * alpha * ww - rr
@@ -504,34 +503,35 @@
     beta = ss / rr
     curve = (sw - alpha * (ww - alpha * wz)) + 2.0 * beta * sw + beta * beta * rw
     step = ss / curve
-    coef[0] = alpha + step * (1.0 + beta)
-    coef[1] = step * alpha
+    c1, c2 = (alpha + step * (1.0 + beta))[0:1], (step * alpha)[0:1]
+    c1, c2 = jnp.concatenate([c1] * 4, axis=1), jnp.concatenate([c2] * 4, axis=1)
+    written = []
+    for b in range(CLOSE):
+        rows = slice(b * (TS // CLOSE), (b + 1) * (TS // CLOSE))
+        r, w = pixels[0, rows, :], pixels[1, rows, :]
+        pixels[2, rows, :] = r - c1 * w + c2 * pixels[2, rows, :]
+        guess[rows, :] = guess[rows, :] + c1 * r - c2 * w
+        for k, (source, target) in enumerate(((guess, solution_hbm), (pixels.at[2], residual_hbm))):
+            written.append(pltpu.make_async_copy(source.at[rows], target.at[rows], stores.at[b, k]))
+            written[-1].start()
     for store in written:
         store.wait()
 
 
-def closing(guess_hbm, r_hbm, w_hbm, z_hbm, coef, solution_hbm, residual_hbm, held, made, loads, stores):
-    sources = (r_hbm, w_hbm, z_hbm, guess_hbm)
-    copies = {}
-    for b in range(CLOSE):
-        rows = slice(b * (TS // CLOSE), (b + 1) * (TS // CLOSE))
-        for k, source in enumerate(sources):
-            copies[b, k] = pltpu.make_async_copy(source.at[rows], held.at[k, rows], loads.at[b, k])
-            copies[b, k].start()
-    c1, c2 = coef[0, 0:1, 0:1], coef[1, 0:1, 0:1]
-    writes = []
-    for b in range(CLOSE):
-        rows = slice(b * (TS // CLOSE), (b + 1) * (TS // CLOSE))
-        for k in range(4):
-            copies[b, k].wait()
-        r, w = held[0, rows, :], held[1, rows, :]
-        made[1, rows, :] = r - c1 * w + c2 * held[2, rows, :]
-        made[0, rows, :] = held[3, rows, :] + c1 * r - c2 * w
-        for k, target in enumerate((solution_hbm, residual_hbm)):
-            writes.append(pltpu.make_async_copy(made.at[k, rows], target.at[rows], stores.at[b, k]))
-            writes[-1].start()
-    for write in writes:
-        write.wait()
+def hand_over(solution_in, residual_in, solution_out, residual_out, held, loads, sems):
+    arrays = ((solution_in, solution_out), (residual_in, residual_out))
+    spots = [(b, k, slice(b * (TS // PARTS), (b + 1) * (TS // PARTS))) for b in range(PARTS) for k in range(2)]
+    copies = []
+    for b, k, rows in spots:
+        copies.append(pltpu.make_async_copy(arrays[k][0].at[rows], held.at[k, rows], loads.at[b, k]))
+        copies[-1].start()
+    stores = []
+    for copy, (b, k, rows) in zip(copies, spots):
+        copy.wait()
+        stores.append(pltpu.make_async_copy(held.at[k, rows], arrays[k][1].at[rows], sems.at[b, k]))
+        stores[-1].start()
+    for store in stores:
+        store.wait()
 
 
 def on_device(n_wide, n_narrow, frames, anchor, shift, guess):
@@ -539,11 +539,11 @@
     image = jax.ShapeDtypeStruct((TS, TS), F32)
     dma = pltpu.SemaphoreType.DMA
     n_a, n_b = 2 * n_narrow, n_wide // 2
-    r, w, z, coef = pl.pallas_call(
+    made = pl.pallas_call(
         functools.partial(kernel, n_wide, n_narrow),
-        out_shape=(image, image, image, jax.ShapeDtypeStruct((2, 8, 128), F32)),
+        out_shape=(image, image),
         in_specs=[hbm, vmem, vmem, hbm, hbm],
-        out_specs=(hbm, hbm, hbm, vmem),
+        out_specs=(hbm, hbm),
         scratch_shapes=[
             pltpu.VMEM((TS, TS), F32),
             pltpu.VMEM((3, TS, TS), F32),
@@ -563,20 +563,20 @@
             pltpu.VMEM((4, 4, 16, 128), F32),
             pltpu.VMEM((n_a, 8, 128), F32),
             pltpu.VMEM((n_b, 8, 128), F32),
-            dma((4, 8)), dma((4, 8)), dma((2,)), dma((2,)), dma((3,)), dma((3,)),
+            dma((4, 8)), dma((4, 8)), dma((2,)), dma((2,)), dma((3,)), dma((CLOSE, 2)),
             dma((n_a,)), dma((n_a,)), dma((n_b,)), dma((n_b,)),
         ],
         compiler_params=pltpu.CompilerParams(
             collective_id=0, has_side_effects=True, vmem_limit_bytes=VMEM_BYTES),
     )(frames.reshape(8 * FS, FS), anchor, shift.transpose(0, 2, 1), guess, jnp.asarray(tables()))
     return pl.pallas_call(
-        closing,
+        hand_over,
         out_shape=(image, image),
-        in_specs=[hbm, hbm, hbm, hbm, vmem],
+        in_specs=[hbm, hbm],
         out_specs=(hbm, hbm),
-        scratch_shapes=[pltpu.VMEM((4, TS, TS), F32), pltpu.VMEM((2, TS, TS), F32), dma((CLOSE, 4)), dma((CLOSE, 2))],
+        scratch_shapes=[pltpu.VMEM((2, TS, TS), F32), dma((PARTS, 2)), dma((PARTS, 2))],
         compiler_params=pltpu.CompilerParams(vmem_limit_bytes=VMEM_BYTES),
-    )(guess, r, w, z, coef)
+    )(*made)
 
 
 def solution(mesh):

time: 52.9 us -> 50.8 us (0.960)
  Pallas kernels: 51.4 us -> 49.8 us
    pallas_call x1, Pallas kernels: 3.9 us -> 2.39 us  [on_device(): pl.pallas_call(hand_over, out_shape=(image, image), in_specs=[hbm, hbm],...]
where the time goes in v6:
time: 50.8 us; the launch traced here: 50.6 us
  Pallas kernels  49.8 us (98%)
  between operations  0.8 us (2%)
    pallas_call x1, Pallas kernels, on_device(): pl.pallas_call(functools.partial(kernel, n_wide, n_narrow), out_shape=(im...  47.4 us
    pallas_call x1, Pallas kernels, on_device(): pl.pallas_call(hand_over, out_shape=(image, image), in_specs=[hbm, hbm],...  2.39 us

profile of v6, /device:TPU:1, one launch (start us, length us, event | category | flops | bytes accessed | tf_op | source)
XLA Modules:
  0.0 50.6 jit_solution(16146117872934896261)
XLA Ops:
  0.6 47.4 %shard_map.68 = (f32[512,512]{1,0:T(8,128)}, f32[512,512]{1,0:T(8,128)}) custom-call(f32[1024,128]{1,0:T(8,128)} %bitcast.2, s32[1,256]{1,0:T(1,128)} %anchor.1, s32[1,2,256]{2,1,0:T(2,128)} %bitcast.3, f32[512,512]{1,0:T(8,128)} %guess_hbm.1, f32[3,128,128]{2,1,0:T(8,128)} %constant.2.clone.table_hbm), custom_call_target="tpu_custom_call" | custom-call | tf_op jit(solution)/shard_map/pallas_call | solution.py:542
  48.0 2.4 %shard_map.69 = (f32[512,512]{1,0:T(8,128)}, f32[512,512]{1,0:T(8,128)}) custom-call(f32[512,512]{1,0:T(8,128)} %get-tuple-element.4.solution_in, f32[512,512]{1,0:T(8,128)} %get-tuple-element.5.residual_in), custom_call_target="tpu_custom_call" | custom-call | tf_op jit(solution)/shard_map/pallas_call | solution.py:572

commit v7 on v6

--- a/solution.py
+++ b/solution.py
@@ -256,7 +256,7 @@
 
     settle(0, moves)
 
-    def unfold(v, features=True):
+    def unfold(v):
         unpack(v)
 
         def step(i, carry):
@@ -269,15 +269,12 @@
                 spun = packed if q == 0 else pltpu.roll(packed, 128 - 4 * q, axis=1)
                 x = jnp.where(first | last, spun, raw[q])
                 mid.append(x)
-                if features:
-                    side = pltpu.roll(packed, 126 - 4 * q, axis=1)
-                    prv.append(jnp.where(first, side, pltpu.roll(x, 1, axis=1)))
-                    if q < 3:
-                        nxt.append(jnp.where(last, side, pltpu.roll(x, 127, axis=1)))
+                side = pltpu.roll(packed, 126 - 4 * q, axis=1)
+                prv.append(jnp.where(first, side, pltpu.roll(x, 1, axis=1)))
+                if q < 3:
+                    nxt.append(jnp.where(last, side, pltpu.roll(x, 127, axis=1)))
             for q in range(4):
                 whole[v, q, rows, :] = mid[q]
-            if not features:
-                return carry
             m23, p23 = mid[2] + mid[3], prv[2] + prv[3]
             m123, p123 = mid[1] + m23, prv[1] + p23
             m01, n01 = mid[0] + mid[1], nxt[0] + nxt[1]
@@ -449,12 +446,26 @@
         totals = jnp.broadcast_to(jnp.sum(collect(copies, sums_b), axis=1, keepdims=True), (8, 128))
         return [jnp.broadcast_to(totals[i : i + 1], (8, 128)) for i in range(4)]
 
-    def write_pixels(v):
-        for b in range(4):
-            rows = slice(b * 128, b * 128 + 128)
-            x = jnp.concatenate([whole[v, q, b * 128 + 8 : b * 128 + 136, :] for q in range(4)], axis=1)
+    def write_pixels(source, v, starts=(0, 128, 256, 384), size=128):
+        for start in starts:
+            x = jnp.concatenate([source[v, q, start + 8 : start + 8 + size, :] for q in range(4)], axis=1)
             high, low = halves(x)
-            pixels[v - 1, rows, :] = dot(high, perm[1]) + dot(low, perm[1])
+            pixels[v - 1, start : start + size, :] = dot(high, perm[1]) + dot(low, perm[1])
+
+    def patch_pixels(v):
+        write_pixels(vec, v, (0, TS - 16), 16)
+        edges = [vec[v, 4, 0:PACK, :]]
+        edges += [pltpu.roll(edges[0], 128 - 16 * g, axis=1) for g in range(1, 6)]
+        high, low = halves(jnp.concatenate(edges, axis=0))
+        k_id = lax.broadcasted_iota(jnp.int32, (128, 256), 0)
+        n_id = lax.broadcasted_iota(jnp.int32, (128, 256), 1)
+        left_one = (n_id < 4) & (k_id == 4 * n_id + 1)
+        right_one = (n_id >= 252) & (k_id == 4 * (n_id - 252))
+        place = jnp.where(left_one | right_one, 1.0, 0.0).astype(BF16)
+        outer = (dot(high, place) + dot(low, place))[8 : ROWS - 8]
+        lane = lax.broadcasted_iota(jnp.int32, (TS, 128), 1)
+        pixels[v - 1, :, 0:128] = jnp.where(lane < 4, outer[:, 0:128], pixels[v - 1, :, 0:128])
+        pixels[v - 1, :, 384:512] = jnp.where(lane >= 124, outer[:, 128:256], pixels[v - 1, :, 384:512])
 
     unfold(0)
     mix()
@@ -476,7 +487,7 @@
     rr, rw = fold(1, 1.0, measure_w, 2)
     rw = rw + outer_columns(vec[1, 4, 0:PACK, :] * vec[2, 4, 0:PACK, :])
     moves = exchange(2)
-    write_pixels(1)
+    write_pixels(whole, 1)
     settle(2, moves)
 
     unfold(2)
@@ -491,11 +502,11 @@
     sums = gather_a((rr, rw, ww, wz))
     fold(2, 1.0, no_sums, 0)
     moves = exchange(3)
-    write_pixels(2)
+    write_pixels(whole, 2)
+    write_pixels(vec, 3)
     sums = gather_b(sums)
     settle(3, moves)
-    unfold(3, features=False)
-    write_pixels(3)
+    patch_pixels(3)
     rr, rw, ww, wz = finish_sums(sums)
     alpha = rr / rw
     ss = alpha * alpha * ww - rr

time: 50.8 us -> 50.8 us (level)
  no operation moved by 1% of the time
where the time goes in v7:
time: 50.8 us; the launch traced here: 50.6 us
  Pallas kernels  49.8 us (98%)
  between operations  0.8 us (2%)
    pallas_call x1, Pallas kernels, on_device(): pl.pallas_call(functools.partial(kernel, n_wide, n_narrow), out_shape=(im...  47.4 us
    pallas_call x1, Pallas kernels, on_device(): pl.pallas_call(hand_over, out_shape=(image, image), in_specs=[hbm, hbm],...  2.39 us

profile of v7, /device:TPU:1, one launch (start us, length us, event | category | flops | bytes accessed | tf_op | source)
XLA Modules:
  0.0 50.6 jit_solution(6494888250631220753)
XLA Ops:
  0.6 47.4 %shard_map.68 = (f32[512,512]{1,0:T(8,128)}, f32[512,512]{1,0:T(8,128)}) custom-call(f32[1024,128]{1,0:T(8,128)} %bitcast.2, s32[1,256]{1,0:T(1,128)} %anchor.1, s32[1,2,256]{2,1,0:T(2,128)} %bitcast.3, f32[512,512]{1,0:T(8,128)} %guess_hbm.1, f32[3,128,128]{2,1,0:T(8,128)} %constant.2.clone.table_hbm), custom_call_target="tpu_custom_call" | custom-call | tf_op jit(solution)/shard_map/pallas_call | solution.py:553
  48.0 2.4 %shard_map.69 = (f32[512,512]{1,0:T(8,128)}, f32[512,512]{1,0:T(8,128)}) custom-call(f32[512,512]{1,0:T(8,128)} %get-tuple-element.4.solution_in, f32[512,512]{1,0:T(8,128)} %get-tuple-element.5.residual_in), custom_call_target="tpu_custom_call" | custom-call | tf_op jit(solution)/shard_map/pallas_call | solution.py:583

commit v8 on v7

--- a/solution.py
+++ b/solution.py
@@ -74,17 +74,16 @@
     row = lax.axis_index("narrow")
     left, right = lax.rem(column + n_wide - 1, n_wide), lax.rem(column + 1, n_wide)
     up, down = lax.rem(row + n_narrow - 1, n_narrow), lax.rem(row + 1, n_narrow)
-    core, chip = lax.rem(column, 2), column // 2
-    n_chip = n_wide // 2
 
     def at(w, n):
         return {"wide": w, "narrow": n}
 
     near = [at(right, row), at(left, row), at(column, down), at(column, up),
             at(right, down), at(left, down), at(right, up), at(left, up)]
-    mates_a = [(row + (k // 2), core + (k % 2)) for k in range(1, 2 * n_narrow)]
-    mates_a = [at(chip * 2 + lax.rem(c, 2), lax.rem(r, n_narrow)) for r, c in mates_a]
-    mates_b = [at(lax.rem(chip + k, n_chip) * 2 + core, row) for k in range(1, n_chip)]
+    n_far = n_wide // 8
+    mates_a = [at(lax.rem(column + 8 * (k % n_far), n_wide), lax.rem(row + k // n_far, n_narrow))
+               for k in range(1, n_narrow * n_far)]
+    mates_b = [at((column // 8) * 8 + lax.rem(column + k, 8), row) for k in range(1, 8)]
 
     barrier = pltpu.get_barrier_semaphore()
     everyone = near + mates_a + mates_b
@@ -549,7 +548,7 @@
     vmem, hbm = pl.BlockSpec(memory_space=pltpu.VMEM), pl.BlockSpec(memory_space=pltpu.HBM)
     image = jax.ShapeDtypeStruct((TS, TS), F32)
     dma = pltpu.SemaphoreType.DMA
-    n_a, n_b = 2 * n_narrow, n_wide // 2
+    n_a, n_b = n_narrow * (n_wide // 8), 8
     made = pl.pallas_call(
         functools.partial(kernel, n_wide, n_narrow),
         out_shape=(image, image),

time: 50.8 us -> 51 us (level)
  no operation moved by 1% of the time
where the time goes in v8:
time: 51 us; the launch traced here: 50.8 us
  Pallas kernels  50 us (98%)
  between operations  0.8 us (2%)
    pallas_call x1, Pallas kernels, on_device(): pl.pallas_call(functools.partial(kernel, n_wide, n_narrow), out_shape=(im...  47.6 us
    pallas_call x1, Pallas kernels, on_device(): pl.pallas_call(hand_over, out_shape=(image, image), in_specs=[hbm, hbm],...  2.39 us

profile of v8, /device:TPU:1, one launch (start us, length us, event | category | flops | bytes accessed | tf_op | source)
XLA Modules:
  0.0 50.8 jit_solution(60391035944044334)
XLA Ops:
  0.6 47.6 %shard_map.68 = (f32[512,512]{1,0:T(8,128)}, f32[512,512]{1,0:T(8,128)}) custom-call(f32[1024,128]{1,0:T(8,128)} %bitcast.2, s32[1,256]{1,0:T(1,128)} %anchor.1, s32[1,2,256]{2,1,0:T(2,128)} %bitcast.3, f32[512,512]{1,0:T(8,128)} %guess_hbm.1, f32[3,128,128]{2,1,0:T(8,128)} %constant.2.clone.table_hbm), custom_call_target="tpu_custom_call" | custom-call | tf_op jit(solution)/shard_map/pallas_call | solution.py:552
  48.2 2.4 %shard_map.69 = (f32[512,512]{1,0:T(8,128)}, f32[512,512]{1,0:T(8,128)}) custom-call(f32[512,512]{1,0:T(8,128)} %get-tuple-element.4.solution_in, f32[512,512]{1,0:T(8,128)} %get-tuple-element.5.residual_in), custom_call_target="tpu_custom_call" | custom-call | tf_op jit(solution)/shard_map/pallas_call | solution.py:582
